TPU v7x, 256 devices: a whole 4x4x8 slice. The times are simulated.
256 devices in a mesh: dp: 8 (over x, core), expert: 32 (over z, y).
Axes of the slice: x: 4, y: 4, z: 8, core: 2. Of those that a mesh axis runs over, the one named last changes fastest.
Arguments:
- tokens: bfloat16 [32768, 2048], P(('dp', 'expert')), may hold values from -6 to 6
- grad_out: bfloat16 [32768, 2048], P(('dp', 'expert')), may hold values from -6 to 6
- expert_ids: int32 [32768, 8], P(('dp', 'expert')), may hold values from 0 to 127, all different within a row; in each aligned block of 128 rows (0 to 127, 128 to 255, ...) at most 16 rows name the same one
- gate_probs: bfloat16 [32768, 8], P(('dp', 'expert')), may hold values from 0.019897461 to 0.5
- w_gate: bfloat16 [32, 2048, 768], P('expert'), may hold values from -0.125 to 0.125
- w_up: bfloat16 [32, 2048, 768], P('expert'), may hold values from -0.125 to 0.125
- w_down: bfloat16 [32, 768, 2048], P('expert'), may hold values from -0.21875 to 0.21875
Outputs:
- input_grad: bfloat16 [32768, 2048], P(('dp', 'expert'))
- gate_grad: float32 [32768, 8], P(('dp', 'expert'))
- gate_weight_grad: bfloat16 [32, 2048, 768], P('expert', 'dp')
- up_weight_grad: bfloat16 [32, 2048, 768], P('expert', 'dp')
- down_weight_grad: bfloat16 [32, 768, 2048], P('expert', None, 'dp')
Inputs may be any that keep to these rules, and one draw needn't show every extreme that they name: `expert_ids`: each row names 8 different experts; among the rows of one device no expert is named more than 16 times, a bound that some block reaches.
All inputs are finite; a program needn't handle non-finite values.
Results may differ from a plain program's by a relative error of at most 0.019.
Values may be sent and summed in bfloat16 or wider, within the bound.
No kernel may reach another device: no remote copies, remote signals or barrier semaphores. Data moves between devices by JAX's collectives and lax.ppermute only.
A program may use at most 128 MiB of HBM per device.

v0:
```python
import jax
import jax.numpy as jnp
from jax import lax
from jax.sharding import PartitionSpec as P

CAP = 16


def slot_math(x_rows, dy_rows, g_rows, w_gate, w_up, w_down):
    gate_pre = jnp.dot(x_rows, w_gate, preferred_element_type=jnp.float32)
    up_pre = jnp.dot(x_rows, w_up, preferred_element_type=jnp.float32)
    sig = jax.nn.sigmoid(gate_pre)
    act = gate_pre * sig
    hidden = (act * up_pre).astype(jnp.bfloat16)
    gvals = g_rows.astype(jnp.float32)[:, None]
    scaled_dy = (gvals * dy_rows.astype(jnp.float32)).astype(jnp.bfloat16)
    back = lax.dot_general(
        dy_rows, w_down, (((1,), (1,)), ((), ())), preferred_element_type=jnp.float32
    )
    router = jnp.sum(back * hidden.astype(jnp.float32), axis=1)
    dhidden = gvals * back
    d_up = (dhidden * act).astype(jnp.bfloat16)
    d_gatepre = (dhidden * up_pre * (sig * (1.0 + gate_pre * (1.0 - sig)))).astype(jnp.bfloat16)
    dx_rows = lax.dot_general(
        d_gatepre, w_gate, (((1,), (1,)), ((), ())), preferred_element_type=jnp.float32
    )
    dx_rows = dx_rows + lax.dot_general(
        d_up, w_up, (((1,), (1,)), ((), ())), preferred_element_type=jnp.float32
    )
    return (scaled_dy, hidden, d_gatepre, d_up, dx_rows, router)


def on_device(tokens, grad_out, expert_ids, gate_probs, w_gate, w_up, w_down):
    tok_dev, width = tokens.shape
    topk = expert_ids.shape[1]
    groups = lax.axis_size("expert")
    slots = groups * CAP
    assigns = tok_dev * topk
    flat_ids = expert_ids.reshape(-1)
    hits = (flat_ids[:, None] == jnp.arange(groups, dtype=jnp.int32)[None, :]).astype(jnp.int32)
    rank = jnp.sum((jnp.cumsum(hits, axis=0) - hits) * hits, axis=1)
    slot = jnp.where(flat_ids < groups, flat_ids * CAP + rank, slots)
    assign_table = (
        jnp.full((slots + 1,), assigns, jnp.int32)
        .at[slot]
        .set(jnp.arange(assigns, dtype=jnp.int32))[:slots]
    )
    live_slot = assign_table < assigns
    safe_assign = jnp.minimum(assign_table, assigns - 1)
    token_of_slot = safe_assign // topk
    zero_b = jnp.zeros((), jnp.bfloat16)
    send_x = jnp.where(live_slot[:, None], tokens[token_of_slot], zero_b).reshape(
        groups, CAP, width
    )
    send_dy = jnp.where(live_slot[:, None], grad_out[token_of_slot], zero_b).reshape(
        groups, CAP, width
    )
    send_g = jnp.where(live_slot, gate_probs.reshape(-1)[safe_assign], zero_b).reshape(groups, CAP)
    recv_x, recv_dy, recv_g = (
        lax.all_to_all(send_x, "expert", split_axis=0, concat_axis=0, tiled=True),
        lax.all_to_all(send_dy, "expert", split_axis=0, concat_axis=0, tiled=True),
        lax.all_to_all(send_g, "expert", split_axis=0, concat_axis=0, tiled=True),
    )
    x_rows = recv_x.reshape(slots, width)
    dy_rows = recv_dy.reshape(slots, width)
    g_rows = recv_g.reshape(slots)
    wg = w_gate[0]
    wu = w_up[0]
    wd = w_down[0]
    hid_units = wg.shape[1]
    scaled_dy, hidden, d_gatepre, d_up, dx_rows, router = slot_math(
        x_rows, dy_rows, g_rows, wg, wu, wd
    )
    back_dx, back_dg = (
        lax.all_to_all(
            dx_rows.reshape(groups, CAP, width).astype(jnp.bfloat16),
            "expert",
            split_axis=0,
            concat_axis=0,
            tiled=True,
        ).astype(jnp.float32),
        lax.all_to_all(
            router.reshape(groups, CAP).astype(jnp.bfloat16),
            "expert",
            split_axis=0,
            concat_axis=0,
            tiled=True,
        ).astype(jnp.float32),
    )
    dump = jnp.where(live_slot, token_of_slot, tok_dev)
    input_grad = (
        jnp.zeros((tok_dev + 1, width), jnp.float32)
        .at[dump]
        .add(back_dx.reshape(slots, width))[:tok_dev]
    )
    dump_assign = jnp.where(live_slot, assign_table, assigns)
    gate_grad = (
        jnp.zeros((assigns + 1,), jnp.float32).at[dump_assign].add(back_dg.reshape(slots))[:assigns]
    )
    term_g = lax.dot_general(
        x_rows, d_gatepre, (((0,), (0,)), ((), ())), preferred_element_type=jnp.float32
    )
    term_u = lax.dot_general(
        x_rows, d_up, (((0,), (0,)), ((), ())), preferred_element_type=jnp.float32
    )
    term_d = lax.dot_general(
        scaled_dy, hidden, (((0,), (0,)), ((), ())), preferred_element_type=jnp.float32
    )
    summed = lax.psum_scatter(
        jnp.concatenate([term_g, term_u, term_d], axis=1).astype(jnp.bfloat16),
        "dp",
        scatter_dimension=0,
        tiled=True,
    ).astype(jnp.float32)
    grad_g = summed[:, :hid_units]
    grad_u = summed[:, hid_units : 2 * hid_units]
    grad_d = summed[:, 2 * hid_units :].T
    return (
        input_grad.astype(jnp.bfloat16),
        gate_grad.reshape(tok_dev, topk),
        grad_g.astype(jnp.bfloat16)[None],
        grad_u.astype(jnp.bfloat16)[None],
        grad_d.astype(jnp.bfloat16)[None],
    )


def solution(mesh):
    in_specs = (
        P(("dp", "expert"), None),
        P(("dp", "expert"), None),
        P(("dp", "expert"), None),
        P(("dp", "expert"), None),
        P("expert", None, None),
        P("expert", None, None),
        P("expert", None, None),
    )
    out_specs = (
        P(("dp", "expert"), None),
        P(("dp", "expert"), None),
        P("expert", "dp", None),
        P("expert", "dp", None),
        P("expert", None, "dp"),
    )
    return jax.shard_map(
        on_device, mesh=mesh, in_specs=in_specs, out_specs=out_specs, check_vma=False
    )
```

profile of v0, /device:TPU:2, one launch (start us, length us, event | category | flops | bytes accessed | tf_op | source)
XLA Modules:
  0.0 284.2 jit_solution(11816482873670202455)
XLA Ops:
  7.2 0.0 copy-start
  7.2 0.8 broadcast_compare_fusion
  8.0 0.8 broadcast_multiply_fusion
  8.8 0.8 copy.26
  9.6 0.1 eq.29
  9.7 0.1 eq.25
  9.8 0.1 copy.24
  9.9 0.1 lt.58
  10.0 0.1 copy.25
  10.1 0.1 mul.61
  10.2 9.0 %reduce-window.6 = s32[32,8,128]{2,1,0:T(8,128)S(1)} reduce-window(s32[32,8,128]{2,1,0:T(8,128)S(1)} %fusion.20, s32[]{:T(128)} %constant.21.clone.1), window={size=1x1x128 pad=0_0x0_0x127_0}, to_apply=%region_0.0 | reduce-window | flops 4161536 | bytes 262148 | tf_op jit(solution)/shard_map/reduce-window
  19.3 0.1 slice.42
  19.4 0.1 copy.28
  19.5 0.1 copy.29
  19.6 0.1 broadcast_add_fusion
  19.8 4.3 %scatter_custom_fusion = s32[513]{0:T(1024)S(1)} fusion(s32[1024]{0:T(1024)S(1)} %bitcast.72, s32[1024]{0:T(1024)S(1)} %iota.11, s32[]{:T(128)} %constant.18.clone.1), kind=kCustom, calls=%fused_computation.65 | custom fusion | bytes 2056 | tf_op jit(solution)/shard_map/scatter | solution.py:46
  24.1 0.8 copy.30
  24.9 0.1 reshape.164
  25.1 3.5 %gather_fusion = bf16[512]{0:T(512)(128)(2,1)S(1)} fusion(bf16[1024]{0:T(1024)(128)(2,1)S(1)} %reshape.164, s32[1024]{0:T(1024)S(1)} %get-tuple-element.35), kind=kCustom, calls=%fused_computation | custom fusion | bytes 4096 | tf_op jit(solution)/shard_map/gather | solution.py:58
  28.6 0.7 select_n.83
  29.3 11.5 %all-to-all-start = ((bf16[32,1,16]{2,1,0:T(2,128)(2,1)}), bf16[32,1,16]{2,1,0:T(2,128)(2,1)S(1)}, u32[]{:S(2)}, u32[]{:S(2)}) async-start(bf16[32,1,16]{2,1,0:T(2,128)(2,1)} %select_n.83), calls=%async_computation | async-start | bytes 32768 | tf_op jit(solution)/shard_map/all_to_all | solution.py:62
  40.8 0.1 lt.63
  40.9 6.4 %gather_fusion.1 = bf16[512,2048]{1,0:T(8,128)(2,1)} fusion(bf16[128,2048]{1,0:T(8,128)(2,1)} %param.8, s32[1024]{0:T(1024)S(1)} %get-tuple-element.34), kind=kCustom, calls=%fused_computation.1 | custom fusion | bytes 4196352 | tf_op jit(solution)/shard_map/gather | solution.py:55
  47.3 6.3 %gather_fusion.2 = bf16[512,2048]{1,0:T(8,128)(2,1)} fusion(bf16[128,2048]{1,0:T(8,128)(2,1)} %param.7, s32[1024]{0:T(1024)S(1)} %get-tuple-element.34), kind=kCustom, calls=%fused_computation.2 | custom fusion | bytes 4196352 | tf_op jit(solution)/shard_map/gather | solution.py:52
  53.6 4.6 %broadcast_select_fusion.1 = (bf16[32,16,2048]{2,1,0:T(8,128)(2,1)}, bf16[32,16,2048]{2,1,0:T(8,128)(2,1)}) fusion(bf16[32,16,2048]{2,1,0:T(8,128)(2,1)} %bitcast.62, pred[32,16]{1,0:T(8,128)(4,1)S(1)} %lt.63, bf16[32,16,2048]{2,1,0:T(8,128)(2,1)} %bitcast.63), kind=kLoop, calls=%fused_computation.26 | loop fusion | flops 2097152 | bytes 8389120 | tf_op jit(solution)/shard_map/jit(_where)/select_n | solution.py:55
  58.2 0.0 all-to-all-done
  58.2 59.8 %all_to_all.27 = bf16[32,16,2048]{2,1,0:T(8,128)(2,1)} all-to-all(bf16[32,16,2048]{2,1,0:T(8,128)(2,1)} %get-tuple-element.33), channel_id=1, replica_groups=mesh['dp'=8,'expert'=32] {'expert'}, dimensions={0} | all-to-all | bytes 4194304 | tf_op jit(solution)/shard_map/all_to_all | solution.py:60
  118.0 5.7 %all-to-all-start.1 = ((bf16[32,16,2048]{2,1,0:T(8,128)(2,1)}), bf16[32,16,2048]{2,1,0:T(8,128)(2,1)}, u32[]{:S(2)}, u32[]{:S(2)}) async-start(bf16[32,16,2048]{2,1,0:T(8,128)(2,1)} %get-tuple-element.32), calls=%async_computation.1 | async-start | bytes 4194304 | tf_op jit(solution)/shard_map/all_to_all | solution.py:61
  123.7 0.2 reduce-scatter.2.cloned.1.call-start
  124.0 0.1 convert_reduce_fusion.1
  124.0 0.1 reshape.170
  124.1 5.6 %fusion.8 = f32[512,768]{1,0:T(8,128)} fusion(bf16[512,2048]{1,0:T(8,128)(2,1)} %bitcast.64, bf16[1,2048,768]{2,1,0:T(8,128)(2,1)} %param.12), kind=kOutput, calls=%fused_computation.20 | convolution fusion | flops 1610612736 | bytes 6815744 | tf_op jit(solution)/shard_map/dot_general | solution.py:11
  129.7 0.0 copy-done
  129.7 0.0 copy-done.1
  129.7 3.0 %fusion.4 = f32[512,768]{1,0:T(8,128)} fusion(bf16[512,2048]{1,0:T(8,128)(2,1)S(1)} %bitcast.65, bf16[1,2048,768]{2,1,0:T(8,128)(2,1)S(1)} %copy-done), kind=kOutput, calls=%fused_computation.16 | convolution fusion | flops 1610612736 | bytes 6815744 | tf_op jit(solution)/shard_map/dot_general | solution.py:10
  132.7 39.8 %all-to-all-done.1 = bf16[32,16,2048]{2,1,0:T(8,128)(2,1)} async-done(((bf16[32,16,2048]{2,1,0:T(8,128)(2,1)}), bf16[32,16,2048]{2,1,0:T(8,128)(2,1)}, u32[]{:S(2)}, u32[]{:S(2)}) %all-to-all-start.1) | async-done | bytes 2097184 | tf_op jit(solution)/shard_map/all_to_all | solution.py:61
  172.5 6.0 %multiply_reduce_fusion = (bf16[512]{0:T(512)(128)(2,1)S(1)}, bf16[512,768]{1,0:T(8,128)(2,1)S(1)}, bf16[512,768]{1,0:T(8,128)(2,1)S(1)}, bf16[512,768]{1,0:T(8,128)(2,1)S(1)}) fusion(f32[512,768]{1,0:T(8,128)} %fusion.8, f32[512,768]{1,0:T(8,128)} %fusion.4, f32[512]{0:T(512)S(1)} %reshape.170, bf16[512,2048]{1,0:T(8,128)(2,1)} %bitcast.5, ...), kind=kOutput, calls=%fused_computation.27 | convolution fusion | flops 1618083328 | bytes 10750976 | tf_op jit(solution)/shard_map/dot_general | solution.py:17
  178.5 0.0 copy-start.4
  178.5 0.0 copy-start.6
  178.5 0.0 copy-start.2
  178.5 4.1 %convolution_convert_fusion = bf16[2048,768]{0,1:T(8,128)(2,1)S(1)} fusion(bf16[512,768]{1,0:T(8,128)(2,1)S(1)} %get-tuple-element.21, bf16[512,2048]{1,0:T(8,128)(2,1)} %bitcast.5, f32[512]{0:T(512)S(1)} %reshape.170), kind=kOutput, calls=%fused_computation.11 | convolution fusion | flops 1615331328 | bytes 6031360 | tf_op jit(solution)/shard_map/dot_general | solution.py:106
  182.6 0.0 copy-done.4
  182.7 1.8 convolution_convert_fusion.1
  184.5 1.8 convolution_convert_fusion.2
  186.4 4.5 %pad_maximum_fusion = bf16[2048,2304]{0,1:T(8,128)(2,1)} fusion(bf16[2048,768]{0,1:T(8,128)(2,1)S(1)} %convolution_convert_fusion, bf16[2048,768]{0,1:T(8,128)(2,1)S(1)} %convolution_convert_fusion.1, bf16[2048,768]{0,1:T(8,128)(2,1)S(1)} %convolution_convert_fusion.2), kind=kLoop, calls=%fused_computation.6 | loop fusion | flops 28311552 | bytes 18874368 | tf_op jit(solution)/shard_map/concatenate | solution.py:110
  190.9 0.0 reduce-scatter.2.cloned.1.call-update
  190.9 0.7 convert_element_type.90
  191.6 6.1 %all-to-all-start.4 = ((bf16[32,1,16]{2,1,0:T(2,128)(2,1)}), bf16[32,1,16]{2,1,0:T(2,128)(2,1)S(1)}, u32[]{:S(2)}, u32[]{:S(2)}) async-start(bf16[32,1,16]{2,1,0:T(2,128)(2,1)} %convert_element_type.90), calls=%async_computation.4 | async-start | bytes 32768 | tf_op jit(solution)/shard_map/all_to_all | solution.py:82
  197.7 0.0 copy-start.3
  197.7 3.1 %fusion.2 = f32[512,2048]{1,0:T(8,128)S(1)} fusion(bf16[512,768]{1,0:T(8,128)(2,1)} %copy-done.6, bf16[1,2048,768]{2,1,0:T(8,128)(2,1)S(1)} %copy-done), kind=kOutput, calls=%fused_computation.14 | convolution fusion | flops 1610612736 | bytes 8126464 | tf_op jit(solution)/shard_map/dot_general | solution.py:24
  200.9 3.2 %add_convert_fusion = bf16[512,2048]{1,0:T(8,128)(2,1)} fusion(f32[512,2048]{1,0:T(8,128)S(1)} %fusion.2, bf16[512,768]{1,0:T(8,128)(2,1)S(1)} %copy-done.5, bf16[1,2048,768]{2,1,0:T(8,128)(2,1)S(1)} %copy-done.3), kind=kOutput, calls=%fused_computation.10 | convolution fusion | flops 1612709888 | bytes 10223616 | tf_op jit(solution)/shard_map/dot_general | solution.py:27
  204.1 3.0 %all-to-all-done.4 = bf16[32,1,16]{2,1,0:T(2,128)(2,1)S(1)} async-done(((bf16[32,1,16]{2,1,0:T(2,128)(2,1)}), bf16[32,1,16]{2,1,0:T(2,128)(2,1)S(1)}, u32[]{:S(2)}, u32[]{:S(2)}) %all-to-all-start.4) | async-done | bytes 1056 | tf_op jit(solution)/shard_map/all_to_all | solution.py:82
  207.2 6.7 %all-to-all-start.3 = ((bf16[32,16,2048]{2,1,0:T(8,128)(2,1)}), bf16[32,16,2048]{2,1,0:T(8,128)(2,1)}, u32[]{:S(2)}, u32[]{:S(2)}) async-start(bf16[32,16,2048]{2,1,0:T(8,128)(2,1)} %bitcast.68), calls=%async_computation.3 | async-start | bytes 4194304 | tf_op jit(solution)/shard_map/all_to_all | solution.py:75
  213.8 0.1 convert_reduce_fusion
  213.9 0.1 reshape.218
  214.0 3.9 %scatter_custom_fusion.2 = f32[1025]{0:T(1024)S(1)} fusion(s32[512]{0:T(512)S(1)} %get-tuple-element.22, f32[512]{0:T(512)S(1)} %reshape.218, f32[]{:T(128)} %constant.17.clone.1), kind=kCustom, calls=%fused_computation.54 | custom fusion | flops 512 | bytes 4104 | tf_op jit(solution)/shard_map/scatter-add | solution.py:98
  217.8 0.1 reshape.169
  217.9 0.7 copy.33
  218.6 42.5 %all-to-all-done.3 = bf16[32,16,2048]{2,1,0:T(8,128)(2,1)} async-done(((bf16[32,16,2048]{2,1,0:T(8,128)(2,1)}), bf16[32,16,2048]{2,1,0:T(8,128)(2,1)}, u32[]{:S(2)}, u32[]{:S(2)}) %all-to-all-start.3) | async-done | bytes 2097184 | tf_op jit(solution)/shard_map/all_to_all | solution.py:75
  261.1 9.1 %scatter_custom_fusion.1 = f32[129,2048]{1,0:T(8,128)} fusion(s32[512]{0:T(512)S(1)} %get-tuple-element.30, bf16[512,2048]{1,0:T(8,128)(2,1)} %bitcast.17, f32[]{:T(128)} %constant.17.clone.1), kind=kCustom, calls=%fused_computation.7 | custom fusion | flops 2097152 | bytes 3153924 | tf_op jit(solution)/shard_map/scatter-add | solution.py:94
  270.2 2.1 slice.61
  272.3 2.2 slice_bitcast_fusion
  274.5 1.9 copy.34
  276.4 0.9 copy.35
  (18 shorter events, 0.1 us)
Async XLA Ops:
  7.2 122.6 %copy-start = (bf16[1,2048,768]{2,1,0:T(8,128)(2,1)S(1)}, bf16[1,2048,768]{2,1,0:T(8,128)(2,1)}, u32[]{:S(2)}) copy-start(bf16[1,2048,768]{2,1,0:T(8,128)(2,1)} %param.11) | copy-start | bytes 9437188
  29.3 28.9 %all-to-all-start = ((bf16[32,1,16]{2,1,0:T(2,128)(2,1)}), bf16[32,1,16]{2,1,0:T(2,128)(2,1)S(1)}, u32[]{:S(2)}, u32[]{:S(2)}) async-start(bf16[32,1,16]{2,1,0:T(2,128)(2,1)} %select_n.83), calls=%async_computation | async-start | bytes 32768 | tf_op jit(solution)/shard_map/all_to_all | solution.py:62
  118.0 54.5 %all-to-all-start.1 = ((bf16[32,16,2048]{2,1,0:T(8,128)(2,1)}), bf16[32,16,2048]{2,1,0:T(8,128)(2,1)}, u32[]{:S(2)}, u32[]{:S(2)}) async-start(bf16[32,16,2048]{2,1,0:T(8,128)(2,1)} %get-tuple-element.32), calls=%async_computation.1 | async-start | bytes 4194304 | tf_op jit(solution)/shard_map/all_to_all | solution.py:61
  123.7 148.5 %reduce-scatter.2.cloned.1.call-start = ((), (), s32[]{:S(2)}) async-start(), calls=%async_computation.6 | async-start | bytes 10616832 | tf_op jit(solution)/shard_map/reduce_scatter | solution.py:109
  124.1 5.6 %copy-start.1 = (bf16[32,16,2048]{2,1,0:T(8,128)(2,1)S(1)}, bf16[32,16,2048]{2,1,0:T(8,128)(2,1)}, u32[]{:S(2)}) copy-start(bf16[32,16,2048]{2,1,0:T(8,128)(2,1)} %all_to_all.27) | copy-start | bytes 6291460
  178.5 4.1 %copy-start.4 = (bf16[512,768]{1,0:T(8,128)(2,1)}, bf16[512,768]{1,0:T(8,128)(2,1)S(1)}, u32[]{:S(2)}) copy-start(bf16[512,768]{1,0:T(8,128)(2,1)S(1)} %get-tuple-element.25) | copy-start | bytes 2359300
  178.5 6.0 %copy-start.6 = (bf16[512,768]{1,0:T(8,128)(2,1)}, bf16[512,768]{1,0:T(8,128)(2,1)S(1)}, u32[]{:S(2)}) copy-start(bf16[512,768]{1,0:T(8,128)(2,1)S(1)} %get-tuple-element.24) | copy-start | bytes 2359300
  178.5 4.1 %copy-start.2 = (bf16[32,16,2048]{2,1,0:T(8,128)(2,1)S(1)}, bf16[32,16,2048]{2,1,0:T(8,128)(2,1)}, u32[]{:S(2)}) copy-start(bf16[32,16,2048]{2,1,0:T(8,128)(2,1)} %all_to_all.27) | copy-start | bytes 6291460
  191.6 15.6 %all-to-all-start.4 = ((bf16[32,1,16]{2,1,0:T(2,128)(2,1)}), bf16[32,1,16]{2,1,0:T(2,128)(2,1)S(1)}, u32[]{:S(2)}, u32[]{:S(2)}) async-start(bf16[32,1,16]{2,1,0:T(2,128)(2,1)} %convert_element_type.90), calls=%async_computation.4 | async-start | bytes 32768 | tf_op jit(solution)/shard_map/all_to_all | solution.py:82
  197.7 3.1 %copy-start.3 = (bf16[1,2048,768]{2,1,0:T(8,128)(2,1)S(1)}, bf16[1,2048,768]{2,1,0:T(8,128)(2,1)}, u32[]{:S(2)}) copy-start(bf16[1,2048,768]{2,1,0:T(8,128)(2,1)} %param.12) | copy-start | bytes 9437188
  197.7 3.1 %copy-start.5 = (bf16[512,768]{1,0:T(8,128)(2,1)S(1)}, bf16[512,768]{1,0:T(8,128)(2,1)}, u32[]{:S(2)}) copy-start(bf16[512,768]{1,0:T(8,128)(2,1)} %copy-done.4) | copy-start | bytes 2359300
  207.2 53.9 %all-to-all-start.3 = ((bf16[32,16,2048]{2,1,0:T(8,128)(2,1)}), bf16[32,16,2048]{2,1,0:T(8,128)(2,1)}, u32[]{:S(2)}, u32[]{:S(2)}) async-start(bf16[32,16,2048]{2,1,0:T(8,128)(2,1)} %bitcast.68), calls=%async_computation.3 | async-start | bytes 4194304 | tf_op jit(solution)/shard_map/all_to_all | solution.py:75
Sparse Core Ops, SparseCore 0:
  191.0 54.9 reduce-scatter.1
where the time goes:
time: 285 us; the launch traced here: 284 us
  waiting for transfers between devices  85.3 us (30%)
  blocking collectives  59.8 us (21%)
  other arithmetic  33 us (12%)
  local copies, waits for them, and re-layouts  32.7 us (11%)
  starting transfers between devices  30.2 us (11%)
  matrix products  28.7 us (10%)
  between operations  14.3 us (5%)
    all_to_all x1, blocking collectives, on_device(): lax.all_to_all(send_x, 'expert', split_axis=0, concat_axis=0, tiled=True)  59.8 us
    all_to_all x1, waiting for transfers between devices, on_device(): lax.all_to_all(dx_rows.reshape(groups, CAP, width).astype(jnp.bfloat16),...  42.5 us
    all_to_all x1, waiting for transfers between devices, on_device(): lax.all_to_all(send_dy, 'expert', split_axis=0, concat_axis=0, tiled=True)  39.8 us
    all_to_all x1, starting transfers between devices, on_device(): lax.all_to_all(send_g, 'expert', split_axis=0, concat_axis=0, tiled=True)  11.5 us
    another operation x3, other arithmetic  9.15 us
    scatter-add x1, other arithmetic, on_device(): input_grad = jnp.zeros((tok_dev + 1, width), jnp.float32).at[dump].add(ba...  9.14 us
    all_to_all x1, starting transfers between devices, on_device(): lax.all_to_all(dx_rows.reshape(groups, CAP, width).astype(jnp.bfloat16),...  6.66 us
    gather x1, local copies, waits for them, and re-layouts, on_device(): grad_out[token_of_slot]  6.4 us
  transfers between devices with their start and end apart: 5, of which 3 were waited for; matrix products, arithmetic and copies ran while one was open for 17% of the time, Pallas kernels for 0%

commit v1 on v0

v1 whole, which is shorter than its diff:
```python
import functools
import jax
import jax.numpy as jnp
from jax import lax
from jax.experimental import pallas as pl
from jax.experimental.pallas import tpu as pltpu
from jax.sharding import PartitionSpec as P

CAP = 16
LANES = 128
BF = jnp.bfloat16
F32 = jnp.float32
VMEM_LIMIT = 56 * 1024 * 1024


def mm(a, b):
    return jnp.dot(a, b, preferred_element_type=F32)


def mm_nt(a, b):
    return lax.dot_general(a, b, (((1,), (1,)), ((), ())), preferred_element_type=F32)


def params(vmem=VMEM_LIMIT):
    return pltpu.CompilerParams(vmem_limit_bytes=vmem)


def cost(flops, nbytes):
    return pl.CostEstimate(flops=flops, bytes_accessed=nbytes, transcendentals=0)


def route_kernel(groups, ids_ref, probs_ref, tok_ref, dy_ref, out_ref, s_ref, sg_ref):
    topk, tok_dev = ids_ref.shape

    @pl.when(pl.program_id(0) == 0)
    def _():
        ids = ids_ref[...]
        probs = probs_ref[...].astype(F32)
        expert = lax.broadcasted_iota(jnp.int32, (groups, tok_dev), 0)
        hits = jnp.zeros((groups, tok_dev), F32)
        gate = jnp.zeros((groups, tok_dev), F32)
        for k in range(topk):
            hit = ids[k : k + 1] == expert
            hits = jnp.where(hit, 1.0, hits)
            gate = jnp.where(hit, probs[k : k + 1], gate)
        row = lax.broadcasted_iota(jnp.int32, (tok_dev, tok_dev), 0)
        col = lax.broadcasted_iota(jnp.int32, (tok_dev, tok_dev), 1)
        before = jnp.where(row < col, 1.0, 0.0).astype(BF)
        rank = mm(hits.astype(BF), before)
        rank = jnp.where(hits > 0.0, rank, -1.0).astype(jnp.int32)
        slot = lax.broadcasted_iota(jnp.int32, (groups, CAP, tok_dev), 1)
        sel = rank[:, None, :] == slot
        s_ref[...] = jnp.where(sel, 1.0, 0.0).reshape(groups * CAP, tok_dev).astype(BF)
        sg_ref[...] = (
            jnp.where(sel, jnp.broadcast_to(gate[:, None, :], sel.shape), 0.0)
            .reshape(groups * CAP, tok_dev)
            .astype(BF)
        )

    cols = tok_ref.shape[1]
    x = mm(s_ref[...], tok_ref[...]).astype(BF)
    out_ref[:, :CAP, :] = x.reshape(groups, CAP, cols)
    gy = mm(sg_ref[...], dy_ref[...]).astype(BF)
    out_ref[:, CAP:, :] = gy.reshape(groups, CAP, cols)


def route(ids, probs, tokens, grad_out, groups):
    tok_dev, width = tokens.shape
    topk = ids.shape[0]
    slots = groups * CAP
    steps = 4
    cols = width // steps
    const = lambda j: (0, 0)
    return pl.pallas_call(
        functools.partial(route_kernel, groups),
        grid=(steps,),
        in_specs=[
            pl.BlockSpec((topk, tok_dev), const),
            pl.BlockSpec((topk, tok_dev), const),
            pl.BlockSpec((tok_dev, cols), lambda j: (0, j)),
            pl.BlockSpec((tok_dev, cols), lambda j: (0, j)),
        ],
        out_specs=[
            pl.BlockSpec((groups, 2 * CAP, cols), lambda j: (0, 0, j)),
            pl.BlockSpec((slots, tok_dev), const),
        ],
        out_shape=[
            jax.ShapeDtypeStruct((groups, 2 * CAP, width), BF),
            jax.ShapeDtypeStruct((slots, tok_dev), BF),
        ],
        scratch_shapes=[pltpu.VMEM((slots, tok_dev), BF)],
        compiler_params=params(),
        cost_estimate=cost(4 * slots * tok_dev * width, 4 * (slots + tok_dev) * width),
        name="route",
    )(ids, probs, tokens, grad_out)


def mm_tn(a, b):
    return lax.dot_general(a, b, (((0,), (0,)), ((), ())), preferred_element_type=F32)


def expert_kernel(
    recv_hbm, wg_hbm, wu_hbm, wd_hbm, dx_hbm, dw_hbm, x_s, gy_s, wg_s, wu_s, wd_s, dx_s, dw_s, in_sems, out_sems
):
    groups, _, width = recv_hbm.shape
    rows = groups * CAP
    parts = dw_hbm.shape[0]
    loads = [
        pltpu.make_async_copy(recv_hbm.at[:, :CAP, :], x_s, in_sems.at[0]),
        pltpu.make_async_copy(wg_hbm, wg_s, in_sems.at[1]),
        pltpu.make_async_copy(wu_hbm, wu_s, in_sems.at[2]),
        pltpu.make_async_copy(recv_hbm.at[:, CAP:, :], gy_s, in_sems.at[3]),
        pltpu.make_async_copy(wd_hbm, wd_s, in_sems.at[4]),
    ]
    for c in loads:
        c.start()
    stores = []

    def store(src, dst):
        c = pltpu.make_async_copy(src, dst, out_sems.at[len(stores)])
        c.start()
        stores.append(c)

    def weight_part(w, rows_v, units):
        dw_s[w] = mm_tn(rows_v, units).astype(BF).reshape(dw_s.shape[1:])
        store(dw_s.at[w], dw_hbm.at[:, w])

    loads[0].wait()
    loads[1].wait()
    x = x_s[...].reshape(rows, width)
    a = mm(x, wg_s[...])
    loads[2].wait()
    u = mm(x, wu_s[...])
    s = jax.nn.sigmoid(a)
    act = a * s
    fa = u * (s * (1.0 + a * (1.0 - s)))
    h = (act * u).astype(BF)
    loads[3].wait()
    gy = gy_s[...].reshape(rows, width)
    weight_part(0, gy, h)
    loads[4].wait()
    dh = mm_nt(gy, wd_s[...])
    da = (dh * fa).astype(BF)
    du = (dh * act).astype(BF)
    r = jnp.sum(dh * h.astype(F32), axis=1, keepdims=True)
    dx_s[:, width:] = jnp.broadcast_to(r, (rows, LANES)).astype(BF)
    weight_part(1, x, da)
    weight_part(2, x, du)
    cut = width // 2
    for lo, hi, end in ((0, cut, cut), (cut, width, width + LANES)):
        dx = mm_nt(da, wg_s[lo:hi, :]) + mm_nt(du, wu_s[lo:hi, :])
        dx_s[:, lo:hi] = dx.astype(BF)
        store(dx_s.at[:, lo:end], dx_hbm.at[:, lo:end])
    for c in stores:
        c.wait()


def expert_pass(recv, wg, wu, wd, parts):
    groups, _, width = recv.shape
    rows = groups * CAP
    hid = wg.shape[1]
    part = width // parts
    hbm = pl.BlockSpec(memory_space=pl.ANY)
    return pl.pallas_call(
        expert_kernel,
        in_specs=[hbm] * 4,
        out_specs=[hbm] * 2,
        out_shape=[
            jax.ShapeDtypeStruct((rows, width + LANES), BF),
            jax.ShapeDtypeStruct((parts, 3, part, hid), BF),
        ],
        scratch_shapes=[
            pltpu.VMEM((groups, CAP, width), BF),
            pltpu.VMEM((groups, CAP, width), BF),
            pltpu.VMEM(wg.shape, BF),
            pltpu.VMEM(wu.shape, BF),
            pltpu.VMEM(wd.shape, BF),
            pltpu.VMEM((rows, width + LANES), BF),
            pltpu.VMEM((3, parts, part, hid), BF),
            pltpu.SemaphoreType.DMA((5,)),
            pltpu.SemaphoreType.DMA((5,)),
        ],
        compiler_params=params(),
        cost_estimate=cost(16 * rows * width * hid, 2 * (3 * rows * width + 6 * width * hid)),
        name="expert_pass",
    )(recv, wg, wu, wd)


def unpack_kernel(sum_ref, g_ref, u_ref, d_ref):
    d_ref[0] = sum_ref[0, 0].T
    g_ref[0] = sum_ref[0, 1]
    u_ref[0] = sum_ref[0, 2]


def unpack(total):
    _, _, part, hid = total.shape
    return pl.pallas_call(
        unpack_kernel,
        out_shape=[
            jax.ShapeDtypeStruct((1, part, hid), BF),
            jax.ShapeDtypeStruct((1, part, hid), BF),
            jax.ShapeDtypeStruct((1, hid, part), BF),
        ],
        compiler_params=params(),
        name="unpack",
    )(total)


def combine_kernel(width, s_ref, ids_ref, probs_ref, back_ref, dx_ref, gg_ref):
    groups = s_ref.shape[0] // CAP
    topk, tok_dev = ids_ref.shape
    s = s_ref[...]
    dx_ref[...] = mm(s.T, back_ref[:, :width]).astype(BF)
    r = back_ref[:, width:].astype(F32) * s.astype(F32)
    r = jnp.sum(r.reshape(groups, CAP, tok_dev), axis=1)
    ids = ids_ref[...]
    expert = lax.broadcasted_iota(jnp.int32, (groups, tok_dev), 0)
    for k in range(topk):
        v = jnp.sum(jnp.where(expert == ids[k : k + 1], r, 0.0), axis=0, keepdims=True)
        gg_ref[k : k + 1] = v / probs_ref[k : k + 1].astype(F32)


def combine(s, ids, probs, back):
    slots, tok_dev = s.shape
    width = back.shape[1] - LANES
    return pl.pallas_call(
        functools.partial(combine_kernel, width),
        out_shape=[
            jax.ShapeDtypeStruct((tok_dev, width), BF),
            jax.ShapeDtypeStruct(ids.shape, F32),
        ],
        compiler_params=params(),
        cost_estimate=cost(2 * slots * tok_dev * width, 2 * (slots + tok_dev) * width),
        name="combine",
    )(s, ids, probs, back)


def exchange(rows):
    return lax.all_to_all(rows, "expert", split_axis=0, concat_axis=0, tiled=True)


def on_device(tokens, grad_out, expert_ids, gate_probs, w_gate, w_up, w_down):
    groups = lax.axis_size("expert")
    parts = lax.axis_size("dp")
    ids, probs = expert_ids.T, gate_probs.T
    send, sel = route(ids, probs, tokens, grad_out, groups)
    recv = exchange(send)
    dx, dw = expert_pass(recv, w_gate[0], w_up[0], w_down[0], parts)
    slots = dx.shape[0]
    total = lax.psum_scatter(dw, "dp", scatter_dimension=0, tiled=True)
    back = exchange(dx.reshape(groups, CAP, -1)).reshape(slots, -1)
    input_grad, gate_grad = combine(sel, ids, probs, back)
    return input_grad, gate_grad.T, *unpack(total)


def solution(mesh):
    row = P(("dp", "expert"), None)
    per_expert = P("expert", None, None)
    return jax.shard_map(
        on_device,
        mesh=mesh,
        in_specs=(row, row, row, row, per_expert, per_expert, per_expert),
        out_specs=(row, row, P("expert", "dp", None), P("expert", "dp", None), P("expert", None, "dp")),
        check_vma=False,
    )
```

time: 285 us -> 213 us (0.75)
  blocking collectives: 59.8 us -> 167 us
  waiting for transfers between devices: 85.3 us -> 0.02 us
  other arithmetic: 33 us -> 0 us
  local copies, waits for them, and re-layouts: 32.7 us -> 1.6 us
  Pallas kernels: 0 us -> 30.3 us
  starting transfers between devices: 30.2 us -> 0.04 us
  matrix products: 28.7 us -> 0 us
    all_to_all x1 -> x2, blocking collectives: 59.8 us -> 167 us  [exchange(): lax.all_to_all(rows, 'expert', split_axis=0, concat_axis=0, tiled=True)]
    all_to_all x4 -> x0, waiting for transfers between devices: 85.3 us -> none  [the longest x1 42.5 us: on_device(): lax.all_to_all(dx_rows.reshape(groups, CAP, width).astype(jnp.bfloat16),...]
    pallas_call x0 -> x4, Pallas kernels: none -> 30.3 us  [the longest x1 19.8 us: expert_pass(): pl.pallas_call(expert_kernel, in_specs=[hbm] * 4, out_specs=[hbm] * 2, ou...]
    all_to_all x4 -> x0, starting transfers between devices: 30 us -> none  [the longest x1 11.5 us: on_device(): lax.all_to_all(send_g, 'expert', split_axis=0, concat_axis=0, tiled=True)]
    dot_general x8 -> x0, matrix products: 28.7 us -> none  [the longest x1 5.95 us: slot_math(): lax.dot_general(dy_rows, w_down, (((1,), (1,)), ((), ())), preferred_elem...]
    gather x3 -> x0, local copies, waits for them, and re-layouts: 16.3 us -> none  [the longest x1 6.4 us: on_device(): grad_out[token_of_slot]]
    scatter-add x2 -> x0, other arithmetic: 13 us -> none  [the longest x1 9.14 us: on_device(): input_grad = jnp.zeros((tok_dev + 1, width), jnp.float32).at[dump].add(ba...]
    another operation x3 -> x0, other arithmetic: 9.15 us -> none
  transfers between devices with their start and end apart: 5 -> 1, of which waited for: 3 -> 0; matrix products, arithmetic and copies ran while one was open for 17% -> 0% of each run, Pallas kernels for 0% -> 1%
where the time goes in v1:
time: 213 us
  blocking collectives  167 us (78%)
  Pallas kernels  30.3 us (14%)
  between operations  14 us (7%)
    all_to_all x2, blocking collectives, exchange(): lax.all_to_all(rows, 'expert', split_axis=0, concat_axis=0, tiled=True)  167 us
    pallas_call x1, Pallas kernels, expert_pass(): pl.pallas_call(expert_kernel, in_specs=[hbm] * 4, out_specs=[hbm] * 2, ou...  19.8 us
    pallas_call x1, Pallas kernels, route(): pl.pallas_call(functools.partial(route_kernel, groups), grid=(steps,), in...  5.11 us
  transfers between devices with their start and end apart: 1, of which 0 were waited for; matrix products, arithmetic and copies ran while one was open for 0% of the time, Pallas kernels for 1%

profile of v1, /device:TPU:2, one launch (start us, length us, event | category | flops | bytes accessed | tf_op | source)
XLA Modules:
  0.0 212.9 jit_solution(13057936135136260838)
XLA Ops:
  7.2 0.0 reduce-scatter.2.cloned.1.call-start
  7.2 5.1 %route.1 = (bf16[32,32,2048]{2,1,0:T(8,128)(2,1)}, bf16[512,128]{1,0:T(8,128)(2,1)}) custom-call(s32[8,128]{1,0:T(8,128)} %bitcast.10, bf16[8,128]{1,0:T(8,128)(2,1)} %bitcast.12, bf16[128,2048]{1,0:T(8,128)(2,1)} %tok_ref.1, bf16[128,2048]{1,0:T(8,128)(2,1)} %dy_ref.1), custom_call_target="tpu_custom_call" | custom-call | flops 536870912 | bytes 5242880 | tf_op jit(solution)/shard_map/route/pallas_call | solution.py:74
  12.3 107.1 %all_to_all.10.recv_hbm = bf16[32,32,2048]{2,1,0:T(8,128)(2,1)} all-to-all(bf16[32,32,2048]{2,1,0:T(8,128)(2,1)} %get-tuple-element.15), channel_id=1, replica_groups=mesh['dp'=8,'expert'=32] {'expert'}, dimensions={0} | all-to-all | bytes 8388608 | tf_op jit(solution)/shard_map/all_to_all | solution.py:239
  119.4 19.8 %expert_pass.1 = (bf16[512,2176]{1,0:T(8,128)(2,1)}, bf16[8,3,256,768]{3,2,1,0:T(8,128)(2,1)}) custom-call(bf16[32,32,2048]{2,1,0:T(8,128)(2,1)} %all_to_all.10.recv_hbm, bf16[2048,768]{1,0:T(8,128)(2,1)} %bitcast.14, bf16[2048,768]{1,0:T(8,128)(2,1)} %bitcast.15, bf16[768,2048]{1,0:T(8,128)(2,1)} %bitcast.16), custom_call_target="tpu_custom_call" | custom-call | flops 12884901888 | bytes 25165824 | tf_op jit(solution)/shard_map/expert_pass/pallas_call | solution.py:164
  139.2 0.0 copy-start
  139.2 0.0 reduce-scatter.2.cloned.1.call-update
  139.2 1.6 copy-done
  140.8 59.8 %all_to_all.11 = bf16[32,16,2176]{2,1,0:T(8,128)(2,1)} all-to-all(bf16[32,16,2176]{2,1,0:T(8,128)(2,1)S(1)} %bitcast.9), channel_id=1, replica_groups=mesh['dp'=8,'expert'=32] {'expert'}, dimensions={0} | all-to-all | bytes 4456448 | tf_op jit(solution)/shard_map/all_to_all | solution.py:239
  200.6 3.0 %combine.1 = (bf16[128,2048]{1,0:T(8,128)(2,1)}, f32[8,128]{1,0:T(8,128)}) custom-call(bf16[512,128]{1,0:T(8,128)(2,1)} %get-tuple-element.14.s_ref, s32[8,128]{1,0:T(8,128)} %bitcast.11, bf16[8,128]{1,0:T(8,128)(2,1)} %bitcast.13, bf16[512,2176]{1,0:T(8,128)(2,1)} %bitcast.8), custom_call_target="tpu_custom_call" | custom-call | flops 268435456 | bytes 2621440 | tf_op jit(solution)/shard_map/combine/pallas_call | solution.py:226
  203.6 0.0 reduce-scatter.2.cloned.1.call-done.sum_ref
  203.6 2.4 %unpack.1 = (bf16[1,256,768]{2,1,0:T(8,128)(2,1)}, bf16[1,256,768]{2,1,0:T(8,128)(2,1)}, bf16[1,768,256]{2,1,0:T(8,128)(2,1)}) custom-call(bf16[1,3,256,768]{3,2,1,0:T(8,128)(2,1)} %reduce-scatter.2.cloned.1.call-done.sum_ref), custom_call_target="tpu_custom_call" | custom-call | tf_op jit(solution)/shard_map/unpack/pallas_call | solution.py:197
Async XLA Ops:
  7.2 196.5 %reduce-scatter.2.cloned.1.call-start = ((), (), s32[]{:S(2)}) async-start(), calls=%async_computation.3 | async-start | bytes 10616832 | tf_op jit(solution)/shard_map/reduce_scatter | solution.py:250
  139.2 1.6 copy-start
Sparse Core Ops, SparseCore 0:
  139.3 54.5 reduce-scatter.1

commit v2 on v1

--- a/solution.py
+++ b/solution.py
@@ -99,12 +99,26 @@
     return lax.dot_general(a, b, (((0,), (0,)), ((), ())), preferred_element_type=F32)
 
 
+def put_parts(tmp_ref, down, gate, up):
+    part, hid = gate.shape[0] // 2, gate.shape[1]
+    half = hid // 2
+    for c in range(2):
+        cols = slice(c * part, (c + 1) * part)
+        for i in range(2):
+            tmp_ref[c, i, 2] = down[i * half : (i + 1) * half, cols]
+        for lo in range(0, hid, LANES):
+            b, q = lo // part, lo % part
+            rows = slice(c * part + q, c * part + q + LANES)
+            for w, t in ((0, gate), (1, up)):
+                tmp_ref[c, lo // half, w, lo % half : lo % half + LANES] = t[rows, b * part : (b + 1) * part]
+
+
 def expert_kernel(
-    recv_hbm, wg_hbm, wu_hbm, wd_hbm, dx_hbm, dw_hbm, x_s, gy_s, wg_s, wu_s, wd_s, dx_s, dw_s, in_sems, out_sems
+    place_ref, recv_hbm, wg_hbm, wu_hbm, wd_hbm, dx_hbm, own_hbm, other_hbm,
+    x_s, gy_s, wg_s, wu_s, wd_s, dx_s, tmp_s, in_sems, dx_sems, own_sems, other_sems,
 ):
     groups, _, width = recv_hbm.shape
     rows = groups * CAP
-    parts = dw_hbm.shape[0]
     loads = [
         pltpu.make_async_copy(recv_hbm.at[:, :CAP, :], x_s, in_sems.at[0]),
         pltpu.make_async_copy(wg_hbm, wg_s, in_sems.at[1]),
@@ -116,14 +130,10 @@
         c.start()
     stores = []
 
-    def store(src, dst):
-        c = pltpu.make_async_copy(src, dst, out_sems.at[len(stores)])
+    def store(src, dst, sem):
+        c = pltpu.make_async_copy(src, dst, sem)
         c.start()
         stores.append(c)
-
-    def weight_part(w, rows_v, units):
-        dw_s[w] = mm_tn(rows_v, units).astype(BF).reshape(dw_s.shape[1:])
-        store(dw_s.at[w], dw_hbm.at[:, w])
 
     loads[0].wait()
     loads[1].wait()
@@ -136,39 +146,41 @@
     fa = u * (s * (1.0 + a * (1.0 - s)))
     h = (act * u).astype(BF)
     loads[3].wait()
-    gy = gy_s[...].reshape(rows, width)
-    weight_part(0, gy, h)
     loads[4].wait()
-    dh = mm_nt(gy, wd_s[...])
+    dh = mm_nt(gy_s[...].reshape(rows, width), wd_s[...])
     da = (dh * fa).astype(BF)
     du = (dh * act).astype(BF)
     r = jnp.sum(dh * h.astype(F32), axis=1, keepdims=True)
     dx_s[:, width:] = jnp.broadcast_to(r, (rows, LANES)).astype(BF)
-    weight_part(1, x, da)
-    weight_part(2, x, du)
+    core, pair = place_ref[0], width // 4
+    for j in range(4):
+        cols = pl.ds(pl.multiple_of(place_ref[1 + j] * pair, pair), pair)
+        xc = x_s[:, :, cols].reshape(rows, pair)
+        gyc = gy_s[:, :, cols].reshape(rows, pair)
+        put_parts(tmp_s.at[j], mm_tn(h, gyc).astype(BF), mm_tn(xc, da).astype(BF), mm_tn(xc, du).astype(BF))
+        store(tmp_s.at[j, core], own_hbm.at[j], own_sems.at[j])
+        store(tmp_s.at[j, 1 - core], other_hbm.at[j], other_sems.at[j])
     cut = width // 2
-    for lo, hi, end in ((0, cut, cut), (cut, width, width + LANES)):
+    for i, lo, hi, end in ((0, 0, cut, cut), (1, cut, width, width + LANES)):
         dx = mm_nt(da, wg_s[lo:hi, :]) + mm_nt(du, wu_s[lo:hi, :])
         dx_s[:, lo:hi] = dx.astype(BF)
-        store(dx_s.at[:, lo:end], dx_hbm.at[:, lo:end])
+        store(dx_s.at[:, lo:end], dx_hbm.at[:, lo:end], dx_sems.at[i])
     for c in stores:
         c.wait()
 
 
-def expert_pass(recv, wg, wu, wd, parts):
+def expert_pass(place, recv, wg, wu, wd):
     groups, _, width = recv.shape
     rows = groups * CAP
     hid = wg.shape[1]
-    part = width // parts
+    part = width // 8
     hbm = pl.BlockSpec(memory_space=pl.ANY)
+    parts = jax.ShapeDtypeStruct((4, 2, 3, hid // 2, part), BF)
     return pl.pallas_call(
         expert_kernel,
-        in_specs=[hbm] * 4,
-        out_specs=[hbm] * 2,
-        out_shape=[
-            jax.ShapeDtypeStruct((rows, width + LANES), BF),
-            jax.ShapeDtypeStruct((parts, 3, part, hid), BF),
-        ],
+        in_specs=[pl.BlockSpec(memory_space=pltpu.SMEM)] + [hbm] * 4,
+        out_specs=[hbm] * 3,
+        out_shape=[jax.ShapeDtypeStruct((rows, width + LANES), BF), parts, parts],
         scratch_shapes=[
             pltpu.VMEM((groups, CAP, width), BF),
             pltpu.VMEM((groups, CAP, width), BF),
@@ -176,34 +188,71 @@
             pltpu.VMEM(wu.shape, BF),
             pltpu.VMEM(wd.shape, BF),
             pltpu.VMEM((rows, width + LANES), BF),
-            pltpu.VMEM((3, parts, part, hid), BF),
+            pltpu.VMEM((4, 2, 2, 3, hid // 2, part), BF),
             pltpu.SemaphoreType.DMA((5,)),
-            pltpu.SemaphoreType.DMA((5,)),
+            pltpu.SemaphoreType.DMA((2,)),
+            pltpu.SemaphoreType.DMA((4,)),
+            pltpu.SemaphoreType.DMA((4,)),
         ],
         compiler_params=params(),
         cost_estimate=cost(16 * rows * width * hid, 2 * (3 * rows * width + 6 * width * hid)),
         name="expert_pass",
-    )(recv, wg, wu, wd)
-
-
-def unpack_kernel(sum_ref, g_ref, u_ref, d_ref):
-    d_ref[0] = sum_ref[0, 0].T
-    g_ref[0] = sum_ref[0, 1]
-    u_ref[0] = sum_ref[0, 2]
-
-
-def unpack(total):
-    _, _, part, hid = total.shape
+    )(place, recv, wg, wu, wd)
+
+
+def reduce_parts(own, other):
+    swap = lambda t: lax.ppermute(t, "dp", [(i, i ^ 1) for i in range(8)])
+    shift = lambda t, d: lax.ppermute(t, "dp", [(i, (i + 2 * d) % 8) for i in range(8)])
+    add = lambda *t: sum(v.astype(F32) for v in t).astype(BF)
+    other = swap(other)
+    from_left = shift(add(own[0, 0], other[0, 0]), 1)
+    from_right = shift(add(own[0, 1], other[0, 1]), -1)
+    plain_left = shift(add(own[1, 1], other[1, 1]), 1)
+    plain_right = shift(add(own[2, 0], other[2, 0]), -1)
+    sum_left = shift(add(own[1, 0], other[1, 0], from_left), 1)
+    sum_right = shift(add(own[2, 1], other[2, 1], from_right), -1)
+    return own, other, plain_left, plain_right, sum_left, sum_right
+
+
+def finish_kernel(own_ref, other_ref, pl_ref, pr_ref, sl_ref, sr_ref, g_ref, u_ref, d_ref):
+    part = g_ref.shape[1]
+    half = own_ref.shape[3]
+    low = own_ref[0, 0].astype(F32) + other_ref[0, 0].astype(F32)
+    low = (low + pr_ref[...].astype(F32) + sl_ref[...].astype(F32)).astype(BF)
+    high = own_ref[0, 1].astype(F32) + other_ref[0, 1].astype(F32)
+    high = (high + pl_ref[...].astype(F32) + sr_ref[...].astype(F32)).astype(BF)
+    d_ref[0, :half] = low[2]
+    d_ref[0, half:] = high[2]
+    for w, ref in ((0, g_ref), (1, u_ref)):
+        for b in range(2 * half // part):
+            for lo in range(b * part, (b + 1) * part, LANES):
+                src = low[w, lo : lo + LANES] if lo < half else high[w, lo - half : lo - half + LANES]
+                ref[0, lo - b * part : lo - b * part + LANES, b * part : (b + 1) * part] = src
+
+
+def finish(own, other, *recvd):
+    _, _, _, half, part = own.shape
+    hid = 2 * half
+    mine = pl.BlockSpec((1, 2, 3, half, part), lambda i: (3, 0, 0, 0, 0))
+    whole = pl.BlockSpec((3, half, part), lambda i: (0, 0, 0))
+    zero = lambda i: (0, 0, 0)
     return pl.pallas_call(
-        unpack_kernel,
+        finish_kernel,
+        grid=(1,),
+        in_specs=[mine, mine] + [whole] * 4,
+        out_specs=[
+            pl.BlockSpec((1, part, hid), zero),
+            pl.BlockSpec((1, part, hid), zero),
+            pl.BlockSpec((1, hid, part), zero),
+        ],
         out_shape=[
             jax.ShapeDtypeStruct((1, part, hid), BF),
             jax.ShapeDtypeStruct((1, part, hid), BF),
             jax.ShapeDtypeStruct((1, hid, part), BF),
         ],
         compiler_params=params(),
-        name="unpack",
-    )(total)
+        name="finish",
+    )(own, other, *recvd)
 
 
 def combine_kernel(width, s_ref, ids_ref, probs_ref, back_ref, dx_ref, gg_ref):
@@ -241,16 +290,19 @@
 
 def on_device(tokens, grad_out, expert_ids, gate_probs, w_gate, w_up, w_down):
     groups = lax.axis_size("expert")
-    parts = lax.axis_size("dp")
     ids, probs = expert_ids.T, gate_probs.T
     send, sel = route(ids, probs, tokens, grad_out, groups)
     recv = exchange(send)
-    dx, dw = expert_pass(recv, w_gate[0], w_up[0], w_down[0], parts)
+    p = lax.axis_index("dp")
+    x, core = p // 2, p % 2
+    place = jnp.stack([core, (x + 2) % 4, (x + 1) % 4, (x + 3) % 4, x])
+    dx, own, other = expert_pass(place, recv, w_gate[0], w_up[0], w_down[0])
     slots = dx.shape[0]
-    total = lax.psum_scatter(dw, "dp", scatter_dimension=0, tiled=True)
     back = exchange(dx.reshape(groups, CAP, -1)).reshape(slots, -1)
+    grads = finish(*reduce_parts(own, other))
+    sel, *grads = lax.optimization_barrier((sel, *grads))
     input_grad, gate_grad = combine(sel, ids, probs, back)
-    return input_grad, gate_grad.T, *unpack(total)
+    return input_grad, gate_grad.T, *grads
 
 
 def solution(mesh):

time: 213 us -> 197 us (0.925)
  blocking collectives: 167 us -> 0 us
  waiting for transfers between devices: 0.02 us -> 130 us
  starting transfers between devices: 0.04 us -> 26.2 us
  between operations: 14 us -> 0.76 us
  other arithmetic: 0 us -> 4.94 us
    all_to_all x2 -> x0, blocking collectives: 167 us -> none  [exchange(): lax.all_to_all(rows, 'expert', split_axis=0, concat_axis=0, tiled=True)]
    all_to_all x0 -> x2, waiting for transfers between devices: none -> 96.3 us  [exchange(): lax.all_to_all(rows, 'expert', split_axis=0, concat_axis=0, tiled=True)]
    ppermute x0 -> x7, waiting for transfers between devices: none -> 33.9 us  [the longest x6 32.5 us: reduce_parts(): lax.ppermute(t, 'dp', [(i, (i + 2 * d) % 8) for i in range(8)])]
    all_to_all x0 -> x2, starting transfers between devices: none -> 18.4 us  [exchange(): lax.all_to_all(rows, 'expert', split_axis=0, concat_axis=0, tiled=True)]
    ppermute x0 -> x7, starting transfers between devices: none -> 7.76 us  [the longest x6 7.49 us: reduce_parts(): lax.ppermute(t, 'dp', [(i, (i + 2 * d) % 8) for i in range(8)])]
    convert_element_type x0 -> x2, other arithmetic: none -> 4.94 us  [reduce_parts(): add = lambda *t: sum((v.astype(F32) for v in t)).astype(BF)]
  transfers between devices with their start and end apart: 1 -> 9, of which waited for: 0 -> 9; matrix products, arithmetic and copies ran while one was open for 0% -> 3% of each run, Pallas kernels for 1% -> 2%
where the time goes in v2:
time: 197 us; the launch traced here: 196 us
  waiting for transfers between devices  130 us (66%)
  Pallas kernels  30.9 us (16%)
  starting transfers between devices  26.2 us (13%)
  other arithmetic  4.94 us (3%)
  local copies, waits for them, and re-layouts  2.88 us (1%)
    all_to_all x2, waiting for transfers between devices, exchange(): lax.all_to_all(rows, 'expert', split_axis=0, concat_axis=0, tiled=True)  96.3 us
    ppermute x6, waiting for transfers between devices, reduce_parts(): lax.ppermute(t, 'dp', [(i, (i + 2 * d) % 8) for i in range(8)])  32.5 us
    pallas_call x1, Pallas kernels, expert_pass(): pl.pallas_call(expert_kernel, in_specs=[pl.BlockSpec(memory_space=pltpu.S...  19.2 us
    all_to_all x2, starting transfers between devices, exchange(): lax.all_to_all(rows, 'expert', split_axis=0, concat_axis=0, tiled=True)  18.4 us
    ppermute x6, starting transfers between devices, reduce_parts(): lax.ppermute(t, 'dp', [(i, (i + 2 * d) % 8) for i in range(8)])  7.49 us
    pallas_call x1, Pallas kernels, route(): pl.pallas_call(functools.partial(route_kernel, groups), grid=(steps,), in...  5.06 us
    convert_element_type x2, other arithmetic, reduce_parts(): add = lambda *t: sum((v.astype(F32) for v in t)).astype(BF)  4.94 us
  transfers between devices with their start and end apart: 9, of which 9 were waited for; matrix products, arithmetic and copies ran while one was open for 3% of the time, Pallas kernels for 2%

profile of v2, /device:TPU:2, one launch (start us, length us, event | category | flops | bytes accessed | tf_op | source)
XLA Modules:
  0.0 195.9 jit_solution(1514364187584284689)
XLA Ops:
  0.6 5.1 %route.1 = (bf16[32,32,2048]{2,1,0:T(8,128)(2,1)}, bf16[512,128]{1,0:T(8,128)(2,1)}) custom-call(s32[8,128]{1,0:T(8,128)} %bitcast.31, bf16[8,128]{1,0:T(8,128)(2,1)} %bitcast.33, bf16[128,2048]{1,0:T(8,128)(2,1)} %tok_ref.1, bf16[128,2048]{1,0:T(8,128)(2,1)} %dy_ref.1), custom_call_target="tpu_custom_call" | custom-call | flops 536870912 | bytes 5242880 | tf_op jit(solution)/shard_map/route/pallas_call | solution.py:74
  5.7 11.6 %all-to-all-start = ((bf16[32,32,2048]{2,1,0:T(8,128)(2,1)}), bf16[32,32,2048]{2,1,0:T(8,128)(2,1)}, u32[]{:S(2)}, u32[]{:S(2)}) async-start(bf16[32,32,2048]{2,1,0:T(8,128)(2,1)} %get-tuple-element.20), calls=%async_computation | async-start | bytes 8388608 | tf_op jit(solution)/shard_map/all_to_all | solution.py:288
  17.4 0.7 stack.23.place_ref
  18.1 93.6 %all-to-all-done.recv_hbm = bf16[32,32,2048]{2,1,0:T(8,128)(2,1)} async-done(((bf16[32,32,2048]{2,1,0:T(8,128)(2,1)}), bf16[32,32,2048]{2,1,0:T(8,128)(2,1)}, u32[]{:S(2)}, u32[]{:S(2)}) %all-to-all-start) | async-done | bytes 4194336 | tf_op jit(solution)/shard_map/all_to_all | solution.py:288
  111.7 19.2 %expert_pass.1 = (bf16[512,2176]{1,0:T(8,128)(2,1)}, bf16[4,2,3,384,256]{4,3,2,1,0:T(8,128)(2,1)}, bf16[4,2,3,384,256]{4,3,2,1,0:T(8,128)(2,1)}) custom-call(s32[5]{0:T(128)} %stack.23.place_ref, bf16[32,32,2048]{2,1,0:T(8,128)(2,1)} %all-to-all-done.recv_hbm, bf16[2048,768]{1,0:T(8,128)(2,1)} %bitcast.35, bf16[2048,768]{1,0:T(8,128)(2,1)} %bitcast.36, ...), custom_call_target="tpu_custom_call" | custom-call | flops 12884901888 | bytes 25165824 | tf_op jit(solution)/shard_map/expert_pass/pallas_call | solution.py:179
  130.9 0.3 collective-permute-start
  131.2 6.8 %all-to-all-start.1 = ((bf16[32,16,2176]{2,1,0:T(8,128)(2,1)}), bf16[32,16,2176]{2,1,0:T(8,128)(2,1)S(1)}, u32[]{:S(2)}, u32[]{:S(2)}) async-start(bf16[32,16,2176]{2,1,0:T(8,128)(2,1)} %bitcast.30), calls=%async_computation.1 | async-start | bytes 4456448 | tf_op jit(solution)/shard_map/all_to_all | solution.py:288
  138.0 1.4 collective-permute-done.other_ref
  139.4 2.9 %fusion.5 = (bf16[3,384,256]{2,1,0:T(8,128)(2,1)S(1)}, bf16[3,384,256]{2,1,0:T(8,128)(2,1)S(1)}, bf16[3,384,256]{2,1,0:T(8,128)(2,1)S(1)}, bf16[3,384,256]{2,1,0:T(8,128)(2,1)S(1)}) fusion(bf16[4,2,3,384,256]{4,3,2,1,0:T(8,128)(2,1)} %collective-permute-done.other_ref, bf16[4,2,3,384,256]{4,3,2,1,0:T(8,128)(2,1)} %get-tuple-element.21.own_ref), kind=kLoop, calls=%fused_computation.11 | loop fusion | flops 4718592 | bytes 7077888 | tf_op jit(solution)/shard_map/convert_element_type | solution.py:206
  142.3 0.6 collective-permute-start.5
  142.9 1.5 collective-permute-start.3
  144.4 1.3 collective-permute-start.2
  145.7 0.8 collective-permute-start.1
  146.5 12.1 %collective-permute-done.5 = bf16[3,384,256]{2,1,0:T(8,128)(2,1)S(1)} collective-permute-done((bf16[3,384,256]{2,1,0:T(8,128)(2,1)S(1)}, bf16[3,384,256]{2,1,0:T(8,128)(2,1)S(1)}, u32[]{:S(2)}, u32[]{:S(2)}) %collective-permute-start.5) | collective-permute-done | bytes 589856 | tf_op jit(solution)/shard_map/ppermute | solution.py:205
  158.6 1.3 collective-permute-done.3
  159.9 2.0 %fusion = (bf16[3,384,256]{2,1,0:T(8,128)(2,1)S(1)}, bf16[3,384,256]{2,1,0:T(8,128)(2,1)S(1)}) fusion(bf16[3,384,256]{2,1,0:T(8,128)(2,1)S(1)} %collective-permute-done.5, bf16[4,2,3,384,256]{4,3,2,1,0:T(8,128)(2,1)} %collective-permute-done.other_ref, bf16[4,2,3,384,256]{4,3,2,1,0:T(8,128)(2,1)} %get-tuple-element.21.own_ref, ...), kind=kLoop, calls=%fused_computation.1 | loop fusion | flops 3538944 | bytes 4718592 | tf_op jit(solution)/shard_map/convert_element_type | solution.py:206
  161.9 3.4 %collective-permute-start.6 = (bf16[3,384,256]{2,1,0:T(8,128)(2,1)S(1)}, bf16[3,384,256]{2,1,0:T(8,128)(2,1)S(1)}, u32[]{:S(2)}, u32[]{:S(2)}) collective-permute-start(bf16[3,384,256]{2,1,0:T(8,128)(2,1)S(1)} %get-tuple-element.33), channel_id=1, source_target_pairs={{0,192},{32,224},{64,0},{96,32},{128,64},{160,96},{192,128},{224,1... | collective-permute-start | bytes 1769480 | tf_op jit(solution)/shard_map/ppermute | solution.py:205
  165.2 0.0 collective-permute-start.4
  165.2 6.0 %collective-permute-done.2.pr_ref = bf16[3,384,256]{2,1,0:T(8,128)(2,1)S(1)} collective-permute-done((bf16[3,384,256]{2,1,0:T(8,128)(2,1)S(1)}, bf16[3,384,256]{2,1,0:T(8,128)(2,1)S(1)}, u32[]{:S(2)}, u32[]{:S(2)}) %collective-permute-start.2) | collective-permute-done | bytes 589856 | tf_op jit(solution)/shard_map/ppermute | solution.py:205
  171.2 0.0 copy-start.1
  171.2 1.3 collective-permute-done.1.pl_ref
  172.5 0.0 copy-start.2
  172.5 10.6 %collective-permute-done.6.sr_ref = bf16[3,384,256]{2,1,0:T(8,128)(2,1)S(1)} collective-permute-done((bf16[3,384,256]{2,1,0:T(8,128)(2,1)S(1)}, bf16[3,384,256]{2,1,0:T(8,128)(2,1)S(1)}, u32[]{:S(2)}, u32[]{:S(2)}) %collective-permute-start.6) | collective-permute-done | bytes 589856 | tf_op jit(solution)/shard_map/ppermute | solution.py:205
  183.1 0.0 copy-start.3
  183.1 1.3 collective-permute-done.4.sl_ref
  184.3 0.0 copy-done.1
  184.3 0.0 copy-done.2
  184.3 0.0 copy-done.3
  184.4 0.0 copy-start.4
  184.4 0.8 copy-done.4
  185.2 3.6 %finish.1 = (bf16[1,256,768]{2,1,0:T(8,128)(2,1)}, bf16[1,256,768]{2,1,0:T(8,128)(2,1)}, bf16[1,768,256]{2,1,0:T(8,128)(2,1)}) custom-call(bf16[4,2,3,384,256]{4,3,2,1,0:T(8,128)(2,1)} %get-tuple-element.21.own_ref, bf16[4,2,3,384,256]{4,3,2,1,0:T(8,128)(2,1)} %collective-permute-done.other_ref, bf16[3,384,256]{2,1,0:T(8,128)(2,1)} %copy-done.2, ...), custom_call_target="tpu_custom_call" | custom-call | tf_op jit(solution)/shard_map/finish/pallas_call | solution.py:239
  188.8 2.7 %all-to-all-done.1 = bf16[32,16,2176]{2,1,0:T(8,128)(2,1)S(1)} async-done(((bf16[32,16,2176]{2,1,0:T(8,128)(2,1)}), bf16[32,16,2176]{2,1,0:T(8,128)(2,1)S(1)}, u32[]{:S(2)}, u32[]{:S(2)}) %all-to-all-start.1) | async-done | bytes 2228256 | tf_op jit(solution)/shard_map/all_to_all | solution.py:288
  191.5 0.0 copy-start
  191.5 1.4 copy-done
  192.9 3.0 %combine.1 = (bf16[128,2048]{1,0:T(8,128)(2,1)}, f32[8,128]{1,0:T(8,128)}) custom-call(bf16[512,128]{1,0:T(8,128)(2,1)} %get-tuple-element.26.s_ref, s32[8,128]{1,0:T(8,128)} %bitcast.32, bf16[8,128]{1,0:T(8,128)(2,1)} %bitcast.34, bf16[512,2176]{1,0:T(8,128)(2,1)} %bitcast.29), custom_call_target="tpu_custom_call" | custom-call | flops 268435456 | bytes 2621440 | tf_op jit(solution)/shard_map/combine/pallas_call | solution.py:275
Async XLA Ops:
  5.7 106.0 %all-to-all-start = ((bf16[32,32,2048]{2,1,0:T(8,128)(2,1)}), bf16[32,32,2048]{2,1,0:T(8,128)(2,1)}, u32[]{:S(2)}, u32[]{:S(2)}) async-start(bf16[32,32,2048]{2,1,0:T(8,128)(2,1)} %get-tuple-element.20), calls=%async_computation | async-start | bytes 8388608 | tf_op jit(solution)/shard_map/all_to_all | solution.py:288
  130.9 8.5 %collective-permute-start = (bf16[4,2,3,384,256]{4,3,2,1,0:T(8,128)(2,1)}, bf16[4,2,3,384,256]{4,3,2,1,0:T(8,128)(2,1)}, u32[]{:S(2)}, u32[]{:S(2)}) collective-permute-start(bf16[4,2,3,384,256]{4,3,2,1,0:T(8,128)(2,1)} %get-tuple-element.22), channel_id=1, source_target_pairs={{0,32},{32,0},{64,96},{96,64},{128,160},{160,128},{192,224},{224,1... | collective-permute-start | bytes 14155784 | tf_op jit(solution)/shard_map/ppermute | solution.py:204
  131.2 60.3 %all-to-all-start.1 = ((bf16[32,16,2176]{2,1,0:T(8,128)(2,1)}), bf16[32,16,2176]{2,1,0:T(8,128)(2,1)S(1)}, u32[]{:S(2)}, u32[]{:S(2)}) async-start(bf16[32,16,2176]{2,1,0:T(8,128)(2,1)} %bitcast.30), calls=%async_computation.1 | async-start | bytes 4456448 | tf_op jit(solution)/shard_map/all_to_all | solution.py:288
  142.3 16.2 %collective-permute-start.5 = (bf16[3,384,256]{2,1,0:T(8,128)(2,1)S(1)}, bf16[3,384,256]{2,1,0:T(8,128)(2,1)S(1)}, u32[]{:S(2)}, u32[]{:S(2)}) collective-permute-start(bf16[3,384,256]{2,1,0:T(8,128)(2,1)S(1)} %get-tuple-element.35), channel_id=1, source_target_pairs={{0,192},{32,224},{64,0},{96,32},{128,64},{160,96},{192,128},{224,1... | collective-permute-start | bytes 1769480 | tf_op jit(solution)/shard_map/ppermute | solution.py:205
  142.9 16.9 %collective-permute-start.3 = (bf16[3,384,256]{2,1,0:T(8,128)(2,1)S(1)}, bf16[3,384,256]{2,1,0:T(8,128)(2,1)S(1)}, u32[]{:S(2)}, u32[]{:S(2)}) collective-permute-start(bf16[3,384,256]{2,1,0:T(8,128)(2,1)S(1)} %get-tuple-element.36), channel_id=1, source_target_pairs={{0,64},{32,96},{64,128},{96,160},{128,192},{160,224},{192,0},{224,... | collective-permute-start | bytes 1769480 | tf_op jit(solution)/shard_map/ppermute | solution.py:205
  144.4 26.8 %collective-permute-start.2 = (bf16[3,384,256]{2,1,0:T(8,128)(2,1)S(1)}, bf16[3,384,256]{2,1,0:T(8,128)(2,1)S(1)}, u32[]{:S(2)}, u32[]{:S(2)}) collective-permute-start(bf16[3,384,256]{2,1,0:T(8,128)(2,1)S(1)} %get-tuple-element.37), channel_id=1, source_target_pairs={{0,192},{32,224},{64,0},{96,32},{128,64},{160,96},{192,128},{224,1... | collective-permute-start | bytes 1769480 | tf_op jit(solution)/shard_map/ppermute | solution.py:205
  145.7 26.8 %collective-permute-start.1 = (bf16[3,384,256]{2,1,0:T(8,128)(2,1)S(1)}, bf16[3,384,256]{2,1,0:T(8,128)(2,1)S(1)}, u32[]{:S(2)}, u32[]{:S(2)}) collective-permute-start(bf16[3,384,256]{2,1,0:T(8,128)(2,1)S(1)} %get-tuple-element.38), channel_id=1, source_target_pairs={{0,64},{32,96},{64,128},{96,160},{128,192},{160,224},{192,0},{224,... | collective-permute-start | bytes 1769480 | tf_op jit(solution)/shard_map/ppermute | solution.py:205
  161.9 21.2 %collective-permute-start.6 = (bf16[3,384,256]{2,1,0:T(8,128)(2,1)S(1)}, bf16[3,384,256]{2,1,0:T(8,128)(2,1)S(1)}, u32[]{:S(2)}, u32[]{:S(2)}) collective-permute-start(bf16[3,384,256]{2,1,0:T(8,128)(2,1)S(1)} %get-tuple-element.33), channel_id=1, source_target_pairs={{0,192},{32,224},{64,0},{96,32},{128,64},{160,96},{192,128},{224,1... | collective-permute-start | bytes 1769480 | tf_op jit(solution)/shard_map/ppermute | solution.py:205
  165.2 19.1 %collective-permute-start.4 = (bf16[3,384,256]{2,1,0:T(8,128)(2,1)S(1)}, bf16[3,384,256]{2,1,0:T(8,128)(2,1)S(1)}, u32[]{:S(2)}, u32[]{:S(2)}) collective-permute-start(bf16[3,384,256]{2,1,0:T(8,128)(2,1)S(1)} %get-tuple-element.34), channel_id=1, source_target_pairs={{0,64},{32,96},{64,128},{96,160},{128,192},{160,224},{192,0},{224,... | collective-permute-start | bytes 1769480 | tf_op jit(solution)/shard_map/ppermute | solution.py:205
  171.2 13.1 %copy-start.1 = (bf16[3,384,256]{2,1,0:T(8,128)(2,1)}, bf16[3,384,256]{2,1,0:T(8,128)(2,1)S(1)}, u32[]{:S(2)}) copy-start(bf16[3,384,256]{2,1,0:T(8,128)(2,1)S(1)} %collective-permute-done.2.pr_ref) | copy-start | bytes 1769476
  172.5 11.8 %copy-start.2 = (bf16[3,384,256]{2,1,0:T(8,128)(2,1)}, bf16[3,384,256]{2,1,0:T(8,128)(2,1)S(1)}, u32[]{:S(2)}) copy-start(bf16[3,384,256]{2,1,0:T(8,128)(2,1)S(1)} %collective-permute-done.1.pl_ref) | copy-start | bytes 1769476
  183.1 1.3 copy-start.3
  184.4 0.8 copy-start.4
  191.5 1.4 copy-start

commit v3 on v2

--- a/solution.py
+++ b/solution.py
@@ -11,6 +11,7 @@
 BF = jnp.bfloat16
 F32 = jnp.float32
 VMEM_LIMIT = 56 * 1024 * 1024
+SMALL = 16 * 1024 * 1024
 
 
 def mm(a, b):
@@ -211,77 +212,108 @@
     plain_right = shift(add(own[2, 0], other[2, 0]), -1)
     sum_left = shift(add(own[1, 0], other[1, 0], from_left), 1)
     sum_right = shift(add(own[2, 1], other[2, 1], from_right), -1)
-    return own, other, plain_left, plain_right, sum_left, sum_right
-
-
-def finish_kernel(own_ref, other_ref, pl_ref, pr_ref, sl_ref, sr_ref, g_ref, u_ref, d_ref):
+    return partial(own, other, plain_left, plain_right), sum_left, sum_right
+
+
+def partial_kernel(own_ref, other_ref, left_ref, right_ref, out_ref):
+    for i, ref in ((0, right_ref), (1, left_ref)):
+        t = own_ref[0, i].astype(F32) + other_ref[0, i].astype(F32) + ref[...].astype(F32)
+        out_ref[i] = t.astype(BF)
+
+
+def partial(own, other, left, right):
+    _, _, _, half, part = own.shape
+    mine = pl.BlockSpec((1, 2, 3, half, part), lambda i: (3, 0, 0, 0, 0))
+    whole = pl.BlockSpec((3, half, part), lambda i: (0, 0, 0))
+    return pl.pallas_call(
+        partial_kernel,
+        grid=(1,),
+        in_specs=[mine, mine, whole, whole],
+        out_specs=pl.BlockSpec((2, 3, half, part), lambda i: (0, 0, 0, 0)),
+        out_shape=jax.ShapeDtypeStruct((2, 3, half, part), BF),
+        compiler_params=params(SMALL),
+        name="partial",
+    )(own, other, left, right)
+
+
+def finish_kernel(sum_ref, left_ref, right_ref, g_ref, u_ref, d_ref):
     part = g_ref.shape[1]
-    half = own_ref.shape[3]
-    low = own_ref[0, 0].astype(F32) + other_ref[0, 0].astype(F32)
-    low = (low + pr_ref[...].astype(F32) + sl_ref[...].astype(F32)).astype(BF)
-    high = own_ref[0, 1].astype(F32) + other_ref[0, 1].astype(F32)
-    high = (high + pl_ref[...].astype(F32) + sr_ref[...].astype(F32)).astype(BF)
+    half = sum_ref.shape[2]
+    low = (sum_ref[0].astype(F32) + left_ref[...].astype(F32)).astype(BF)
+    high = (sum_ref[1].astype(F32) + right_ref[...].astype(F32)).astype(BF)
     d_ref[0, :half] = low[2]
     d_ref[0, half:] = high[2]
     for w, ref in ((0, g_ref), (1, u_ref)):
-        for b in range(2 * half // part):
-            for lo in range(b * part, (b + 1) * part, LANES):
-                src = low[w, lo : lo + LANES] if lo < half else high[w, lo - half : lo - half + LANES]
-                ref[0, lo - b * part : lo - b * part + LANES, b * part : (b + 1) * part] = src
-
-
-def finish(own, other, *recvd):
-    _, _, _, half, part = own.shape
+        for lo in range(0, 2 * half, LANES):
+            b, q = lo // part, lo % part
+            src = low[w, lo : lo + LANES] if lo < half else high[w, lo - half : lo - half + LANES]
+            ref[0, q : q + LANES, b * part : (b + 1) * part] = src
+
+
+def finish(total, left, right):
+    _, _, half, part = total.shape
     hid = 2 * half
-    mine = pl.BlockSpec((1, 2, 3, half, part), lambda i: (3, 0, 0, 0, 0))
-    whole = pl.BlockSpec((3, half, part), lambda i: (0, 0, 0))
-    zero = lambda i: (0, 0, 0)
     return pl.pallas_call(
         finish_kernel,
-        grid=(1,),
-        in_specs=[mine, mine] + [whole] * 4,
-        out_specs=[
-            pl.BlockSpec((1, part, hid), zero),
-            pl.BlockSpec((1, part, hid), zero),
-            pl.BlockSpec((1, hid, part), zero),
-        ],
         out_shape=[
             jax.ShapeDtypeStruct((1, part, hid), BF),
             jax.ShapeDtypeStruct((1, part, hid), BF),
             jax.ShapeDtypeStruct((1, hid, part), BF),
         ],
-        compiler_params=params(),
+        compiler_params=params(SMALL),
         name="finish",
-    )(own, other, *recvd)
-
-
-def combine_kernel(width, s_ref, ids_ref, probs_ref, back_ref, dx_ref, gg_ref):
+    )(total, left, right)
+
+
+def combine_kernel(s_ref, ids_ref, probs_ref, back_ref, r_ref, dx_ref, gg_ref, st_ref):
     groups = s_ref.shape[0] // CAP
     topk, tok_dev = ids_ref.shape
-    s = s_ref[...]
-    dx_ref[...] = mm(s.T, back_ref[:, :width]).astype(BF)
-    r = back_ref[:, width:].astype(F32) * s.astype(F32)
-    r = jnp.sum(r.reshape(groups, CAP, tok_dev), axis=1)
-    ids = ids_ref[...]
-    expert = lax.broadcasted_iota(jnp.int32, (groups, tok_dev), 0)
-    for k in range(topk):
-        v = jnp.sum(jnp.where(expert == ids[k : k + 1], r, 0.0), axis=0, keepdims=True)
-        gg_ref[k : k + 1] = v / probs_ref[k : k + 1].astype(F32)
+
+    @pl.when(pl.program_id(0) == 0)
+    def _():
+        s = s_ref[...]
+        st_ref[...] = s.T
+        r = r_ref[...].astype(F32) * s.astype(F32)
+        r = jnp.sum(r.reshape(groups, CAP, tok_dev), axis=1)
+        ids = ids_ref[...]
+        expert = lax.broadcasted_iota(jnp.int32, (groups, tok_dev), 0)
+        for k in range(topk):
+            v = jnp.sum(jnp.where(expert == ids[k : k + 1], r, 0.0), axis=0, keepdims=True)
+            gg_ref[k : k + 1] = v / probs_ref[k : k + 1].astype(F32)
+
+    dx_ref[...] = mm(st_ref[...], back_ref[...]).astype(BF)
 
 
 def combine(s, ids, probs, back):
     slots, tok_dev = s.shape
     width = back.shape[1] - LANES
-    return pl.pallas_call(
-        functools.partial(combine_kernel, width),
+    steps = 2
+    cols = width // steps
+    const = lambda j: (0, 0)
+    return pl.pallas_call(
+        combine_kernel,
+        grid=(steps,),
+        in_specs=[
+            pl.BlockSpec(s.shape, const),
+            pl.BlockSpec(ids.shape, const),
+            pl.BlockSpec(ids.shape, const),
+            pl.BlockSpec((slots, cols), lambda j: (0, j)),
+            pl.BlockSpec((slots, LANES), lambda j: (0, width // LANES)),
+        ],
+        out_specs=[pl.BlockSpec((tok_dev, cols), lambda j: (0, j)), pl.BlockSpec(ids.shape, const)],
         out_shape=[
             jax.ShapeDtypeStruct((tok_dev, width), BF),
             jax.ShapeDtypeStruct(ids.shape, F32),
         ],
-        compiler_params=params(),
+        scratch_shapes=[pltpu.VMEM((tok_dev, slots), BF)],
+        compiler_params=params(SMALL),
         cost_estimate=cost(2 * slots * tok_dev * width, 2 * (slots + tok_dev) * width),
         name="combine",
-    )(s, ids, probs, back)
+    )(s, ids, probs, back, back)
+
+
+def exchange(rows):
+    return lax.all_to_all(rows, "expert", split_axis=0, concat_axis=0, tiled=True)
 
 
 def exchange(rows):

time: 197 us -> 194 us (0.985)
  local copies, waits for them, and re-layouts: 2.88 us -> 0.69 us
  waiting for transfers between devices: 130 us -> 132 us
    all_to_all x2, waiting for transfers between devices: 96.3 us -> 99.4 us  [exchange(): lax.all_to_all(rows, 'expert', split_axis=0, concat_axis=0, tiled=True)]
    unnamed x10 -> x8, local copies, waits for them, and re-layouts: 2.2 us -> 0.02 us
    pallas_call x2 -> x3, Pallas kernels: 6.64 us -> 4.77 us  [the longest x1 1.83 us: combine(): pl.pallas_call(combine_kernel, grid=(steps,), in_specs=[pl.BlockSpec(s.sh...]
where the time goes in v3:
time: 194 us; the launch traced here: 193 us
  waiting for transfers between devices  132 us (68%)
  Pallas kernels  29.1 us (15%)
  starting transfers between devices  26.2 us (14%)
  other arithmetic  4.85 us (2%)
    all_to_all x2, waiting for transfers between devices, exchange(): lax.all_to_all(rows, 'expert', split_axis=0, concat_axis=0, tiled=True)  99.4 us
    ppermute x6, waiting for transfers between devices, reduce_parts(): lax.ppermute(t, 'dp', [(i, (i + 2 * d) % 8) for i in range(8)])  31 us
    pallas_call x1, Pallas kernels, expert_pass(): pl.pallas_call(expert_kernel, in_specs=[pl.BlockSpec(memory_space=pltpu.S...  19.3 us
    all_to_all x2, starting transfers between devices, exchange(): lax.all_to_all(rows, 'expert', split_axis=0, concat_axis=0, tiled=True)  18.4 us
    ppermute x6, starting transfers between devices, reduce_parts(): lax.ppermute(t, 'dp', [(i, (i + 2 * d) % 8) for i in range(8)])  7.49 us
    pallas_call x1, Pallas kernels, route(): pl.pallas_call(functools.partial(route_kernel, groups), grid=(steps,), in...  5.07 us
    convert_element_type x2, other arithmetic, reduce_parts(): add = lambda *t: sum((v.astype(F32) for v in t)).astype(BF)  4.85 us
  transfers between devices with their start and end apart: 9, of which 9 were waited for; matrix products, arithmetic and copies ran while one was open for 3% of the time, Pallas kernels for 2%

profile of v3, /device:TPU:2, one launch (start us, length us, event | category | flops | bytes accessed | tf_op | source)
XLA Modules:
  0.0 193.4 jit_solution(11676927459122301007)
XLA Ops:
  0.6 5.1 %route.1 = (bf16[32,32,2048]{2,1,0:T(8,128)(2,1)}, bf16[512,128]{1,0:T(8,128)(2,1)}) custom-call(s32[8,128]{1,0:T(8,128)} %bitcast.31, bf16[8,128]{1,0:T(8,128)(2,1)} %bitcast.33, bf16[128,2048]{1,0:T(8,128)(2,1)} %tok_ref.1, bf16[128,2048]{1,0:T(8,128)(2,1)} %dy_ref.1), custom_call_target="tpu_custom_call" | custom-call | flops 536870912 | bytes 5242880 | tf_op jit(solution)/shard_map/route/pallas_call | solution.py:75
  5.7 11.6 %all-to-all-start = ((bf16[32,32,2048]{2,1,0:T(8,128)(2,1)}), bf16[32,32,2048]{2,1,0:T(8,128)(2,1)}, u32[]{:S(2)}, u32[]{:S(2)}) async-start(bf16[32,32,2048]{2,1,0:T(8,128)(2,1)} %get-tuple-element.20), calls=%async_computation | async-start | bytes 8388608 | tf_op jit(solution)/shard_map/all_to_all | solution.py:320
  17.4 0.7 stack.23.place_ref
  18.1 93.6 %all-to-all-done.recv_hbm = bf16[32,32,2048]{2,1,0:T(8,128)(2,1)} async-done(((bf16[32,32,2048]{2,1,0:T(8,128)(2,1)}), bf16[32,32,2048]{2,1,0:T(8,128)(2,1)}, u32[]{:S(2)}, u32[]{:S(2)}) %all-to-all-start) | async-done | bytes 4194336 | tf_op jit(solution)/shard_map/all_to_all | solution.py:320
  111.7 19.3 %expert_pass.1 = (bf16[512,2176]{1,0:T(8,128)(2,1)}, bf16[4,2,3,384,256]{4,3,2,1,0:T(8,128)(2,1)}, bf16[4,2,3,384,256]{4,3,2,1,0:T(8,128)(2,1)}) custom-call(s32[5]{0:T(128)} %stack.23.place_ref, bf16[32,32,2048]{2,1,0:T(8,128)(2,1)} %all-to-all-done.recv_hbm, bf16[2048,768]{1,0:T(8,128)(2,1)} %bitcast.36, bf16[2048,768]{1,0:T(8,128)(2,1)} %bitcast.37, ...), custom_call_target="tpu_custom_call" | custom-call | flops 12884901888 | bytes 25165824 | tf_op jit(solution)/shard_map/expert_pass/pallas_call | solution.py:180
  131.0 0.3 collective-permute-start
  131.2 6.8 %all-to-all-start.1 = ((bf16[32,16,2176]{2,1,0:T(8,128)(2,1)}), bf16[32,16,2176]{2,1,0:T(8,128)(2,1)S(1)}, u32[]{:S(2)}, u32[]{:S(2)}) async-start(bf16[32,16,2176]{2,1,0:T(8,128)(2,1)} %bitcast.35), calls=%async_computation.1 | async-start | bytes 4456448 | tf_op jit(solution)/shard_map/all_to_all | solution.py:320
  138.0 1.4 collective-permute-done.other_ref
  139.5 0.0 copy-start
  139.5 3.1 %fusion.5 = (bf16[3,384,256]{2,1,0:T(8,128)(2,1)S(1)}, bf16[3,384,256]{2,1,0:T(8,128)(2,1)S(1)}, bf16[3,384,256]{2,1,0:T(8,128)(2,1)S(1)}, bf16[3,384,256]{2,1,0:T(8,128)(2,1)S(1)}) fusion(bf16[4,2,3,384,256]{4,3,2,1,0:T(8,128)(2,1)} %collective-permute-done.other_ref, bf16[4,2,3,384,256]{4,3,2,1,0:T(8,128)(2,1)} %get-tuple-element.21.own_ref), kind=kLoop, calls=%fused_computation.11 | loop fusion | flops 4718592 | bytes 7077888 | tf_op jit(solution)/shard_map/convert_element_type | solution.py:207
  142.6 0.6 collective-permute-start.5
  143.2 1.5 collective-permute-start.3
  144.7 1.3 collective-permute-start.2
  146.0 0.8 collective-permute-start.1
  146.7 12.1 %collective-permute-done.5 = bf16[3,384,256]{2,1,0:T(8,128)(2,1)S(1)} collective-permute-done((bf16[3,384,256]{2,1,0:T(8,128)(2,1)S(1)}, bf16[3,384,256]{2,1,0:T(8,128)(2,1)S(1)}, u32[]{:S(2)}, u32[]{:S(2)}) %collective-permute-start.5) | collective-permute-done | bytes 589856 | tf_op jit(solution)/shard_map/ppermute | solution.py:206
  158.8 1.3 collective-permute-done.3
  160.1 0.0 copy-done
  160.1 1.7 fusion
  161.9 3.4 %collective-permute-start.6 = (bf16[3,384,256]{2,1,0:T(8,128)(2,1)S(1)}, bf16[3,384,256]{2,1,0:T(8,128)(2,1)S(1)}, u32[]{:S(2)}, u32[]{:S(2)}) collective-permute-start(bf16[3,384,256]{2,1,0:T(8,128)(2,1)S(1)} %get-tuple-element.33), channel_id=1, source_target_pairs={{0,192},{32,224},{64,0},{96,32},{128,64},{160,96},{192,128},{224,1... | collective-permute-start | bytes 1769480 | tf_op jit(solution)/shard_map/ppermute | solution.py:206
  165.2 0.0 collective-permute-start.4
  165.2 6.3 %collective-permute-done.2.right_ref = bf16[3,384,256]{2,1,0:T(8,128)(2,1)S(1)} collective-permute-done((bf16[3,384,256]{2,1,0:T(8,128)(2,1)S(1)}, bf16[3,384,256]{2,1,0:T(8,128)(2,1)S(1)}, u32[]{:S(2)}, u32[]{:S(2)}) %collective-permute-start.2) | collective-permute-done | bytes 589856 | tf_op jit(solution)/shard_map/ppermute | solution.py:206
  171.5 1.3 collective-permute-done.1.left_ref
  172.7 1.7 partial.1.sum_ref
  174.5 0.0 copy-start.1
  174.5 0.0 copy-start.2
  174.5 0.0 copy-start.3
  174.5 8.8 %collective-permute-done.6.right_ref = bf16[3,384,256]{2,1,0:T(8,128)(2,1)S(1)} collective-permute-done((bf16[3,384,256]{2,1,0:T(8,128)(2,1)S(1)}, bf16[3,384,256]{2,1,0:T(8,128)(2,1)S(1)}, u32[]{:S(2)}, u32[]{:S(2)}) %collective-permute-start.6) | collective-permute-done | bytes 589856 | tf_op jit(solution)/shard_map/ppermute | solution.py:206
  183.3 1.3 collective-permute-done.4.left_ref
  184.6 1.2 finish.1
  185.8 5.7 %all-to-all-done.1 = bf16[32,16,2176]{2,1,0:T(8,128)(2,1)S(1)} async-done(((bf16[32,16,2176]{2,1,0:T(8,128)(2,1)}), bf16[32,16,2176]{2,1,0:T(8,128)(2,1)S(1)}, u32[]{:S(2)}, u32[]{:S(2)}) %all-to-all-start.1) | async-done | bytes 2228256 | tf_op jit(solution)/shard_map/all_to_all | solution.py:320
  191.5 0.0 copy-done.1
  191.5 0.0 copy-done.2
  191.5 0.0 copy-done.3
  191.5 1.8 combine.1
Async XLA Ops:
  5.7 106.0 %all-to-all-start = ((bf16[32,32,2048]{2,1,0:T(8,128)(2,1)}), bf16[32,32,2048]{2,1,0:T(8,128)(2,1)}, u32[]{:S(2)}, u32[]{:S(2)}) async-start(bf16[32,32,2048]{2,1,0:T(8,128)(2,1)} %get-tuple-element.20), calls=%async_computation | async-start | bytes 8388608 | tf_op jit(solution)/shard_map/all_to_all | solution.py:320
  131.0 8.5 %collective-permute-start = (bf16[4,2,3,384,256]{4,3,2,1,0:T(8,128)(2,1)}, bf16[4,2,3,384,256]{4,3,2,1,0:T(8,128)(2,1)}, u32[]{:S(2)}, u32[]{:S(2)}) collective-permute-start(bf16[4,2,3,384,256]{4,3,2,1,0:T(8,128)(2,1)} %get-tuple-element.22), channel_id=1, source_target_pairs={{0,32},{32,0},{64,96},{96,64},{128,160},{160,128},{192,224},{224,1... | collective-permute-start | bytes 14155784 | tf_op jit(solution)/shard_map/ppermute | solution.py:205
  131.2 60.3 %all-to-all-start.1 = ((bf16[32,16,2176]{2,1,0:T(8,128)(2,1)}), bf16[32,16,2176]{2,1,0:T(8,128)(2,1)S(1)}, u32[]{:S(2)}, u32[]{:S(2)}) async-start(bf16[32,16,2176]{2,1,0:T(8,128)(2,1)} %bitcast.35), calls=%async_computation.1 | async-start | bytes 4456448 | tf_op jit(solution)/shard_map/all_to_all | solution.py:320
  139.5 20.6 %copy-start = (bf16[4,2,3,384,256]{4,3,2,1,0:T(8,128)(2,1)S(1)}, bf16[4,2,3,384,256]{4,3,2,1,0:T(8,128)(2,1)}, u32[]{:S(2)}) copy-start(bf16[4,2,3,384,256]{4,3,2,1,0:T(8,128)(2,1)} %get-tuple-element.21.own_ref) | copy-start | bytes 14155780
  142.6 16.2 %collective-permute-start.5 = (bf16[3,384,256]{2,1,0:T(8,128)(2,1)S(1)}, bf16[3,384,256]{2,1,0:T(8,128)(2,1)S(1)}, u32[]{:S(2)}, u32[]{:S(2)}) collective-permute-start(bf16[3,384,256]{2,1,0:T(8,128)(2,1)S(1)} %get-tuple-element.35), channel_id=1, source_target_pairs={{0,192},{32,224},{64,0},{96,32},{128,64},{160,96},{192,128},{224,1... | collective-permute-start | bytes 1769480 | tf_op jit(solution)/shard_map/ppermute | solution.py:206
  143.2 16.9 %collective-permute-start.3 = (bf16[3,384,256]{2,1,0:T(8,128)(2,1)S(1)}, bf16[3,384,256]{2,1,0:T(8,128)(2,1)S(1)}, u32[]{:S(2)}, u32[]{:S(2)}) collective-permute-start(bf16[3,384,256]{2,1,0:T(8,128)(2,1)S(1)} %get-tuple-element.36), channel_id=1, source_target_pairs={{0,64},{32,96},{64,128},{96,160},{128,192},{160,224},{192,0},{224,... | collective-permute-start | bytes 1769480 | tf_op jit(solution)/shard_map/ppermute | solution.py:206
  144.7 26.8 %collective-permute-start.2 = (bf16[3,384,256]{2,1,0:T(8,128)(2,1)S(1)}, bf16[3,384,256]{2,1,0:T(8,128)(2,1)S(1)}, u32[]{:S(2)}, u32[]{:S(2)}) collective-permute-start(bf16[3,384,256]{2,1,0:T(8,128)(2,1)S(1)} %get-tuple-element.37), channel_id=1, source_target_pairs={{0,192},{32,224},{64,0},{96,32},{128,64},{160,96},{192,128},{224,1... | collective-permute-start | bytes 1769480 | tf_op jit(solution)/shard_map/ppermute | solution.py:206
  146.0 26.8 %collective-permute-start.1 = (bf16[3,384,256]{2,1,0:T(8,128)(2,1)S(1)}, bf16[3,384,256]{2,1,0:T(8,128)(2,1)S(1)}, u32[]{:S(2)}, u32[]{:S(2)}) collective-permute-start(bf16[3,384,256]{2,1,0:T(8,128)(2,1)S(1)} %get-tuple-element.38), channel_id=1, source_target_pairs={{0,64},{32,96},{64,128},{96,160},{128,192},{160,224},{192,0},{224,... | collective-permute-start | bytes 1769480 | tf_op jit(solution)/shard_map/ppermute | solution.py:206
  161.9 21.5 %collective-permute-start.6 = (bf16[3,384,256]{2,1,0:T(8,128)(2,1)S(1)}, bf16[3,384,256]{2,1,0:T(8,128)(2,1)S(1)}, u32[]{:S(2)}, u32[]{:S(2)}) collective-permute-start(bf16[3,384,256]{2,1,0:T(8,128)(2,1)S(1)} %get-tuple-element.33), channel_id=1, source_target_pairs={{0,192},{32,224},{64,0},{96,32},{128,64},{160,96},{192,128},{224,1... | collective-permute-start | bytes 1769480 | tf_op jit(solution)/shard_map/ppermute | solution.py:206
  165.2 19.4 %collective-permute-start.4 = (bf16[3,384,256]{2,1,0:T(8,128)(2,1)S(1)}, bf16[3,384,256]{2,1,0:T(8,128)(2,1)S(1)}, u32[]{:S(2)}, u32[]{:S(2)}) collective-permute-start(bf16[3,384,256]{2,1,0:T(8,128)(2,1)S(1)} %get-tuple-element.34), channel_id=1, source_target_pairs={{0,64},{32,96},{64,128},{96,160},{128,192},{160,224},{192,0},{224,... | collective-permute-start | bytes 1769480 | tf_op jit(solution)/shard_map/ppermute | solution.py:206
  174.5 17.1 %copy-start.1 = (bf16[512,128]{1,0:T(8,128)(2,1)S(1)}, bf16[512,128]{1,0:T(8,128)(2,1)}, u32[]{:S(2)}) copy-start(bf16[512,128]{1,0:T(8,128)(2,1)} %get-tuple-element.26.s_ref) | copy-start | bytes 393220
  174.5 17.0 %copy-start.2 = (s32[128,8]{0,1:T(8,128)S(1)}, s32[128,8]{0,1:T(8,128)}, u32[]{:S(2)}) copy-start(s32[128,8]{0,1:T(8,128)} %param.9) | copy-start | bytes 12292
  174.5 17.0 %copy-start.3 = (bf16[128,8]{0,1:T(8,128)(2,1)S(1)}, bf16[128,8]{0,1:T(8,128)(2,1)}, u32[]{:S(2)}) copy-start(bf16[128,8]{0,1:T(8,128)(2,1)} %param.10) | copy-start | bytes 6148

commit v4 on v3

--- a/solution.py
+++ b/solution.py
@@ -69,7 +69,7 @@
     tok_dev, width = tokens.shape
     topk = ids.shape[0]
     slots = groups * CAP
-    steps = 4
+    steps = 2
     cols = width // steps
     const = lambda j: (0, 0)
     return pl.pallas_call(
@@ -100,23 +100,9 @@
     return lax.dot_general(a, b, (((0,), (0,)), ((), ())), preferred_element_type=F32)
 
 
-def put_parts(tmp_ref, down, gate, up):
-    part, hid = gate.shape[0] // 2, gate.shape[1]
-    half = hid // 2
-    for c in range(2):
-        cols = slice(c * part, (c + 1) * part)
-        for i in range(2):
-            tmp_ref[c, i, 2] = down[i * half : (i + 1) * half, cols]
-        for lo in range(0, hid, LANES):
-            b, q = lo // part, lo % part
-            rows = slice(c * part + q, c * part + q + LANES)
-            for w, t in ((0, gate), (1, up)):
-                tmp_ref[c, lo // half, w, lo % half : lo % half + LANES] = t[rows, b * part : (b + 1) * part]
-
-
-def expert_kernel(
-    place_ref, recv_hbm, wg_hbm, wu_hbm, wd_hbm, dx_hbm, own_hbm, other_hbm,
-    x_s, gy_s, wg_s, wu_s, wd_s, dx_s, tmp_s, in_sems, dx_sems, own_sems, other_sems,
+def rows_kernel(
+    place_ref, recv_hbm, wg_hbm, wu_hbm, wd_hbm, dx_hbm, own_hbm, send_hbm,
+    x_s, gy_s, wg_s, wu_s, wd_s, dx_s, units_s, in_sems, out_sems, cols_sems,
 ):
     groups, _, width = recv_hbm.shape
     rows = groups * CAP
@@ -145,43 +131,45 @@
     s = jax.nn.sigmoid(a)
     act = a * s
     fa = u * (s * (1.0 + a * (1.0 - s)))
-    h = (act * u).astype(BF)
+    units_s[0] = (act * u).astype(BF).reshape(units_s.shape[1:])
     loads[3].wait()
     loads[4].wait()
+    core, part = place_ref[0], width // 8
+    for i, dst in ((0, own_hbm), (1, send_hbm)):
+        for k in range(9):
+            which = 2 * place_ref[1 + k // 2 % 4] + (core if i == 0 else 1 - core)
+            cols = pl.ds(pl.multiple_of(which * part, part), part)
+            src = gy_s if k % 2 else x_s
+            at = slice(k % 3 * part, (k % 3 + 1) * part)
+            store(src.at[:, :, cols], dst.at[3 + k // 3, :, :, at], cols_sems.at[9 * i + k])
     dh = mm_nt(gy_s[...].reshape(rows, width), wd_s[...])
-    da = (dh * fa).astype(BF)
-    du = (dh * act).astype(BF)
+    units_s[1] = (dh * fa).astype(BF).reshape(units_s.shape[1:])
+    units_s[2] = (dh * act).astype(BF).reshape(units_s.shape[1:])
+    store(units_s, own_hbm.at[:3], out_sems.at[2])
+    store(units_s, send_hbm.at[:3], out_sems.at[3])
+    h, da, du = (units_s[i].reshape(rows, units_s.shape[3]) for i in range(3))
     r = jnp.sum(dh * h.astype(F32), axis=1, keepdims=True)
     dx_s[:, width:] = jnp.broadcast_to(r, (rows, LANES)).astype(BF)
-    core, pair = place_ref[0], width // 4
-    for j in range(4):
-        cols = pl.ds(pl.multiple_of(place_ref[1 + j] * pair, pair), pair)
-        xc = x_s[:, :, cols].reshape(rows, pair)
-        gyc = gy_s[:, :, cols].reshape(rows, pair)
-        put_parts(tmp_s.at[j], mm_tn(h, gyc).astype(BF), mm_tn(xc, da).astype(BF), mm_tn(xc, du).astype(BF))
-        store(tmp_s.at[j, core], own_hbm.at[j], own_sems.at[j])
-        store(tmp_s.at[j, 1 - core], other_hbm.at[j], other_sems.at[j])
     cut = width // 2
     for i, lo, hi, end in ((0, 0, cut, cut), (1, cut, width, width + LANES)):
         dx = mm_nt(da, wg_s[lo:hi, :]) + mm_nt(du, wu_s[lo:hi, :])
         dx_s[:, lo:hi] = dx.astype(BF)
-        store(dx_s.at[:, lo:end], dx_hbm.at[:, lo:end], dx_sems.at[i])
+        store(dx_s.at[:, lo:end], dx_hbm.at[:, lo:end], out_sems.at[i])
     for c in stores:
         c.wait()
 
 
-def expert_pass(place, recv, wg, wu, wd):
+def rows_pass(place, recv, wg, wu, wd):
     groups, _, width = recv.shape
     rows = groups * CAP
     hid = wg.shape[1]
-    part = width // 8
     hbm = pl.BlockSpec(memory_space=pl.ANY)
-    parts = jax.ShapeDtypeStruct((4, 2, 3, hid // 2, part), BF)
-    return pl.pallas_call(
-        expert_kernel,
+    pack = jax.ShapeDtypeStruct((6, groups, CAP, hid), BF)
+    return pl.pallas_call(
+        rows_kernel,
         in_specs=[pl.BlockSpec(memory_space=pltpu.SMEM)] + [hbm] * 4,
         out_specs=[hbm] * 3,
-        out_shape=[jax.ShapeDtypeStruct((rows, width + LANES), BF), parts, parts],
+        out_shape=[jax.ShapeDtypeStruct((rows, width + LANES), BF), pack, pack],
         scratch_shapes=[
             pltpu.VMEM((groups, CAP, width), BF),
             pltpu.VMEM((groups, CAP, width), BF),
@@ -189,69 +177,96 @@
             pltpu.VMEM(wu.shape, BF),
             pltpu.VMEM(wd.shape, BF),
             pltpu.VMEM((rows, width + LANES), BF),
-            pltpu.VMEM((4, 2, 2, 3, hid // 2, part), BF),
+            pltpu.VMEM((3, groups, CAP, hid), BF),
             pltpu.SemaphoreType.DMA((5,)),
-            pltpu.SemaphoreType.DMA((2,)),
             pltpu.SemaphoreType.DMA((4,)),
-            pltpu.SemaphoreType.DMA((4,)),
+            pltpu.SemaphoreType.DMA((18,)),
         ],
         compiler_params=params(),
-        cost_estimate=cost(16 * rows * width * hid, 2 * (3 * rows * width + 6 * width * hid)),
-        name="expert_pass",
+        cost_estimate=cost(10 * rows * width * hid, 2 * (3 * rows * width + 3 * width * hid)),
+        name="rows_pass",
     )(place, recv, wg, wu, wd)
 
 
-def reduce_parts(own, other):
+def grad(refs, chunk, w, lo, hi):
+    k = 2 * chunk + (1 if w == 0 else 0)
+    total = 0.0
+    for ref in refs:
+        _, groups, cap, hid = ref.shape
+        part = hid // 3
+        cols = ref[3 + k // 3, :, :, k % 3 * part : (k % 3 + 1) * part].reshape(groups * cap, part)
+        total = total + mm_tn(cols, ref[w, :, :, lo:hi].reshape(groups * cap, hi - lo))
+    return total
+
+
+def first_kernel(*refs):
+    refs, (far_a, far_b, near_b, near_a) = refs[:2], refs[2:]
+    hid = refs[0].shape[3]
+    half = hid // 2
+    for w in range(3):
+        t = grad(refs, 0, w, 0, hid).astype(BF)
+        far_a[w] = t[:, :half]
+        far_b[w] = t[:, half:]
+        near_b[w] = grad(refs, 1, w, half, hid).astype(BF)
+        near_a[w] = grad(refs, 2, w, 0, half).astype(BF)
+
+
+def second_kernel(*refs):
+    refs, (left, right, sum_left, sum_right) = refs[:2], refs[2:]
+    hid = refs[0].shape[3]
+    half = hid // 2
+    for w in range(3):
+        sum_left[w] = (grad(refs, 1, w, 0, half) + left[w].astype(F32)).astype(BF)
+        sum_right[w] = (grad(refs, 2, w, half, hid) + right[w].astype(F32)).astype(BF)
+
+
+def third_kernel(*refs):
+    refs, (left, right, out) = refs[:2], refs[2:]
+    hid = refs[0].shape[3]
+    half = hid // 2
+    for w in range(3):
+        t = grad(refs, 3, w, 0, hid)
+        out[0, w] = (t[:, :half] + right[w].astype(F32)).astype(BF)
+        out[1, w] = (t[:, half:] + left[w].astype(F32)).astype(BF)
+
+
+def part_call(kernel, name, outs, *args):
+    return pl.pallas_call(
+        kernel,
+        out_shape=outs,
+        compiler_params=params(20 * 1024 * 1024),
+        name=name,
+    )(*args)
+
+
+def reduce_parts(own, send):
     swap = lambda t: lax.ppermute(t, "dp", [(i, i ^ 1) for i in range(8)])
     shift = lambda t, d: lax.ppermute(t, "dp", [(i, (i + 2 * d) % 8) for i in range(8)])
-    add = lambda *t: sum(v.astype(F32) for v in t).astype(BF)
-    other = swap(other)
-    from_left = shift(add(own[0, 0], other[0, 0]), 1)
-    from_right = shift(add(own[0, 1], other[0, 1]), -1)
-    plain_left = shift(add(own[1, 1], other[1, 1]), 1)
-    plain_right = shift(add(own[2, 0], other[2, 0]), -1)
-    sum_left = shift(add(own[1, 0], other[1, 0], from_left), 1)
-    sum_right = shift(add(own[2, 1], other[2, 1], from_right), -1)
-    return partial(own, other, plain_left, plain_right), sum_left, sum_right
-
-
-def partial_kernel(own_ref, other_ref, left_ref, right_ref, out_ref):
-    for i, ref in ((0, right_ref), (1, left_ref)):
-        t = own_ref[0, i].astype(F32) + other_ref[0, i].astype(F32) + ref[...].astype(F32)
-        out_ref[i] = t.astype(BF)
-
-
-def partial(own, other, left, right):
-    _, _, _, half, part = own.shape
-    mine = pl.BlockSpec((1, 2, 3, half, part), lambda i: (3, 0, 0, 0, 0))
-    whole = pl.BlockSpec((3, half, part), lambda i: (0, 0, 0))
-    return pl.pallas_call(
-        partial_kernel,
-        grid=(1,),
-        in_specs=[mine, mine, whole, whole],
-        out_specs=pl.BlockSpec((2, 3, half, part), lambda i: (0, 0, 0, 0)),
-        out_shape=jax.ShapeDtypeStruct((2, 3, half, part), BF),
-        compiler_params=params(SMALL),
-        name="partial",
-    )(own, other, left, right)
+    rows = own, swap(send)
+    hid = own.shape[3]
+    part, half = hid // 3, hid // 2
+    piece = jax.ShapeDtypeStruct((3, part, half), BF)
+    far_a, far_b, near_b, near_a = part_call(first_kernel, "first_parts", [piece] * 4, *rows)
+    from_left, from_right = shift(far_a, 1), shift(far_b, -1)
+    plain_left, plain_right = shift(near_b, 1), shift(near_a, -1)
+    sums = part_call(second_kernel, "second_parts", [piece] * 2, *rows, from_left, from_right)
+    mine = jax.ShapeDtypeStruct((2, 3, part, half), BF)
+    total = part_call(third_kernel, "third_parts", mine, *rows, plain_left, plain_right)
+    return total, shift(sums[0], 1), shift(sums[1], -1)
 
 
 def finish_kernel(sum_ref, left_ref, right_ref, g_ref, u_ref, d_ref):
-    part = g_ref.shape[1]
-    half = sum_ref.shape[2]
-    low = (sum_ref[0].astype(F32) + left_ref[...].astype(F32)).astype(BF)
-    high = (sum_ref[1].astype(F32) + right_ref[...].astype(F32)).astype(BF)
-    d_ref[0, :half] = low[2]
-    d_ref[0, half:] = high[2]
-    for w, ref in ((0, g_ref), (1, u_ref)):
-        for lo in range(0, 2 * half, LANES):
-            b, q = lo // part, lo % part
-            src = low[w, lo : lo + LANES] if lo < half else high[w, lo - half : lo - half + LANES]
-            ref[0, q : q + LANES, b * part : (b + 1) * part] = src
+    half = sum_ref.shape[3]
+    for i, ref in ((0, left_ref), (1, right_ref)):
+        t = (sum_ref[i].astype(F32) + ref[...].astype(F32)).astype(BF)
+        cols = slice(i * half, (i + 1) * half)
+        d_ref[0, cols, :] = t[0].T
+        g_ref[0, :, cols] = t[1]
+        u_ref[0, :, cols] = t[2]
 
 
 def finish(total, left, right):
-    _, _, half, part = total.shape
+    _, _, part, half = total.shape
     hid = 2 * half
     return pl.pallas_call(
         finish_kernel,
@@ -287,7 +302,7 @@
 def combine(s, ids, probs, back):
     slots, tok_dev = s.shape
     width = back.shape[1] - LANES
-    steps = 2
+    steps = 1
     cols = width // steps
     const = lambda j: (0, 0)
     return pl.pallas_call(
@@ -328,10 +343,10 @@
     p = lax.axis_index("dp")
     x, core = p // 2, p % 2
     place = jnp.stack([core, (x + 2) % 4, (x + 1) % 4, (x + 3) % 4, x])
-    dx, own, other = expert_pass(place, recv, w_gate[0], w_up[0], w_down[0])
+    dx, *pieces = rows_pass(place, recv, w_gate[0], w_up[0], w_down[0])
     slots = dx.shape[0]
     back = exchange(dx.reshape(groups, CAP, -1)).reshape(slots, -1)
-    grads = finish(*reduce_parts(own, other))
+    grads = finish(*reduce_parts(*pieces))
     sel, *grads = lax.optimization_barrier((sel, *grads))
     input_grad, gate_grad = combine(sel, ids, probs, back)
     return input_grad, gate_grad.T, *grads

time: 194 us -> 187 us (0.964)
  waiting for transfers between devices: 132 us -> 124 us
  Pallas kernels: 29.1 us -> 34.3 us
  other arithmetic: 4.85 us -> 0 us
  local copies, waits for them, and re-layouts: 0.69 us -> 3.01 us
    pallas_call x2 -> x4, Pallas kernels: 21 us -> 27.7 us  [the longest x1 14.4 us: rows_pass(): pl.pallas_call(rows_kernel, in_specs=[pl.BlockSpec(memory_space=pltpu.SME...]
    convert_element_type x2 -> x0, other arithmetic: 4.85 us -> none  [reduce_parts(): add = lambda *t: sum((v.astype(F32) for v in t)).astype(BF)]
    all_to_all x2, waiting for transfers between devices: 99.4 us -> 94.7 us  [exchange(): lax.all_to_all(rows, 'expert', split_axis=0, concat_axis=0, tiled=True)]
    ppermute x6, waiting for transfers between devices: 31 us -> 27.7 us  [reduce_parts(): lax.ppermute(t, 'dp', [(i, (i + 2 * d) % 8) for i in range(8)])]
    unnamed x8, local copies, waits for them, and re-layouts: 0.02 us -> 2.35 us
  transfers between devices with their start and end apart: 9 -> 9, of which waited for: 9 -> 9; matrix products, arithmetic and copies ran while one was open for 3% -> 0% of each run, Pallas kernels for 2% -> 8%
where the time goes in v4:
time: 187 us
  waiting for transfers between devices  124 us (66%)
  Pallas kernels  34.3 us (18%)
  starting transfers between devices  24.9 us (13%)
  local copies, waits for them, and re-layouts  3.01 us (2%)
    all_to_all x2, waiting for transfers between devices, exchange(): lax.all_to_all(rows, 'expert', split_axis=0, concat_axis=0, tiled=True)  94.7 us
    ppermute x6, waiting for transfers between devices, reduce_parts(): lax.ppermute(t, 'dp', [(i, (i + 2 * d) % 8) for i in range(8)])  27.7 us
    all_to_all x2, starting transfers between devices, exchange(): lax.all_to_all(rows, 'expert', split_axis=0, concat_axis=0, tiled=True)  18.6 us
    pallas_call x1, Pallas kernels, rows_pass(): pl.pallas_call(rows_kernel, in_specs=[pl.BlockSpec(memory_space=pltpu.SME...  14.4 us
    pallas_call x3, Pallas kernels, part_call(): pl.pallas_call(kernel, out_shape=outs, compiler_params=params(20 * 1024 *...  13.3 us
    ppermute x6, starting transfers between devices, reduce_parts(): lax.ppermute(t, 'dp', [(i, (i + 2 * d) % 8) for i in range(8)])  6.23 us
    pallas_call x1, Pallas kernels, route(): pl.pallas_call(functools.partial(route_kernel, groups), grid=(steps,), in...  4.01 us
  transfers between devices with their start and end apart: 9, of which 9 were waited for; matrix products, arithmetic and copies ran while one was open for 0% of the time, Pallas kernels for 8%

profile of v4, /device:TPU:2, one launch (start us, length us, event | category | flops | bytes accessed | tf_op | source)
XLA Modules:
  0.0 186.6 jit_solution(9975676557869995968)
XLA Ops:
  0.6 4.0 %route.1 = (bf16[32,32,2048]{2,1,0:T(8,128)(2,1)}, bf16[512,128]{1,0:T(8,128)(2,1)}) custom-call(s32[8,128]{1,0:T(8,128)} %bitcast.15, bf16[8,128]{1,0:T(8,128)(2,1)} %bitcast.17, bf16[128,2048]{1,0:T(8,128)(2,1)} %tok_ref.1, bf16[128,2048]{1,0:T(8,128)(2,1)} %dy_ref.1), custom_call_target="tpu_custom_call" | custom-call | flops 536870912 | bytes 5242880 | tf_op jit(solution)/shard_map/route/pallas_call | solution.py:75
  4.6 11.6 %all-to-all-start = ((bf16[32,32,2048]{2,1,0:T(8,128)(2,1)}), bf16[32,32,2048]{2,1,0:T(8,128)(2,1)}, u32[]{:S(2)}, u32[]{:S(2)}) async-start(bf16[32,32,2048]{2,1,0:T(8,128)(2,1)} %get-tuple-element.26), calls=%async_computation | async-start | bytes 8388608 | tf_op jit(solution)/shard_map/all_to_all | solution.py:335
  16.3 0.7 stack.23.place_ref
  17.0 93.6 %all-to-all-done.recv_hbm = bf16[32,32,2048]{2,1,0:T(8,128)(2,1)} async-done(((bf16[32,32,2048]{2,1,0:T(8,128)(2,1)}), bf16[32,32,2048]{2,1,0:T(8,128)(2,1)}, u32[]{:S(2)}, u32[]{:S(2)}) %all-to-all-start) | async-done | bytes 4194336 | tf_op jit(solution)/shard_map/all_to_all | solution.py:335
  110.6 14.4 %rows_pass.1 = (bf16[512,2176]{1,0:T(8,128)(2,1)}, bf16[6,32,16,768]{3,2,1,0:T(8,128)(2,1)}, bf16[6,32,16,768]{3,2,1,0:T(8,128)(2,1)}) custom-call(s32[5]{0:T(128)} %stack.23.place_ref, bf16[32,32,2048]{2,1,0:T(8,128)(2,1)} %all-to-all-done.recv_hbm, bf16[2048,768]{1,0:T(8,128)(2,1)} %bitcast.20, bf16[2048,768]{1,0:T(8,128)(2,1)} %bitcast.21, ...), custom_call_target="tpu_custom_call" | custom-call | flops 8053063680 | bytes 15728640 | tf_op jit(solution)/shard_map/rows_pass/pallas_call | solution.py:168
  125.0 0.1 collective-permute-start
  125.1 7.0 %all-to-all-start.1 = ((bf16[32,16,2176]{2,1,0:T(8,128)(2,1)}), bf16[32,16,2176]{2,1,0:T(8,128)(2,1)S(1)}, u32[]{:S(2)}, u32[]{:S(2)}) async-start(bf16[32,16,2176]{2,1,0:T(8,128)(2,1)} %bitcast.19), calls=%async_computation.1 | async-start | bytes 4456448 | tf_op jit(solution)/shard_map/all_to_all | solution.py:335
  132.1 1.3 collective-permute-done.refs_1_
  133.3 0.0 copy-start
  133.3 2.3 %copy-done = bf16[6,32,16,768]{3,2,1,0:T(8,128)(2,1)S(1)} copy-done((bf16[6,32,16,768]{3,2,1,0:T(8,128)(2,1)S(1)}, bf16[6,32,16,768]{3,2,1,0:T(8,128)(2,1)}, u32[]{:S(2)}) %copy-start) | copy-done | bytes 4718616
  135.7 5.4 %first_parts.1 = (bf16[3,256,384]{2,1,0:T(8,128)(2,1)S(1)}, bf16[3,256,384]{2,1,0:T(8,128)(2,1)S(1)}, bf16[3,256,384]{2,1,0:T(8,128)(2,1)S(1)}, bf16[3,256,384]{2,1,0:T(8,128)(2,1)S(1)}) custom-call(bf16[6,32,16,768]{3,2,1,0:T(8,128)(2,1)S(1)} %copy-done, bf16[6,32,16,768]{3,2,1,0:T(8,128)(2,1)} %collective-permute-done.refs_1_), custom_call_target="tpu_custom_call" | custom-call | tf_op jit(solution)/shard_map/first_parts/pallas_call | solution.py:234
  141.1 1.6 collective-permute-start.3
  142.6 0.5 collective-permute-start.4
  143.2 1.5 collective-permute-start.1
  144.7 0.5 collective-permute-start.2
  145.2 12.1 %collective-permute-done.3.refs_2_ = bf16[3,256,384]{2,1,0:T(8,128)(2,1)S(1)} collective-permute-done((bf16[3,256,384]{2,1,0:T(8,128)(2,1)S(1)}, bf16[3,256,384]{2,1,0:T(8,128)(2,1)S(1)}, u32[]{:S(2)}, u32[]{:S(2)}) %collective-permute-start.3) | collective-permute-done | bytes 589856 | tf_op jit(solution)/shard_map/ppermute | solution.py:244
  157.3 1.5 collective-permute-done.4.refs_3_
  158.9 4.2 %second_parts.1 = (bf16[3,256,384]{2,1,0:T(8,128)(2,1)S(1)}, bf16[3,256,384]{2,1,0:T(8,128)(2,1)S(1)}) custom-call(bf16[6,32,16,768]{3,2,1,0:T(8,128)(2,1)S(1)} %copy-done, bf16[6,32,16,768]{3,2,1,0:T(8,128)(2,1)} %collective-permute-done.refs_1_, bf16[3,256,384]{2,1,0:T(8,128)(2,1)S(1)} %collective-permute-done.3.refs_2_, ...), custom_call_target="tpu_custom_call" | custom-call | tf_op jit(solution)/shard_map/second_parts/pallas_call | solution.py:234
  163.0 1.3 collective-permute-start.5
  164.3 0.0 copy-start.1
  164.3 0.0 copy-start.2
  164.3 0.0 copy-start.3
  164.3 0.8 collective-permute-start.6
  165.2 4.8 %collective-permute-done.1.refs_2_ = bf16[3,256,384]{2,1,0:T(8,128)(2,1)S(1)} collective-permute-done((bf16[3,256,384]{2,1,0:T(8,128)(2,1)S(1)}, bf16[3,256,384]{2,1,0:T(8,128)(2,1)S(1)}, u32[]{:S(2)}, u32[]{:S(2)}) %collective-permute-start.1) | collective-permute-done | bytes 589856 | tf_op jit(solution)/shard_map/ppermute | solution.py:244
  170.0 1.5 collective-permute-done.2.refs_3_
  171.5 3.8 %third_parts.1.sum_ref = bf16[2,3,256,384]{3,2,1,0:T(8,128)(2,1)S(1)} custom-call(bf16[6,32,16,768]{3,2,1,0:T(8,128)(2,1)S(1)} %copy-done, bf16[6,32,16,768]{3,2,1,0:T(8,128)(2,1)} %collective-permute-done.refs_1_, bf16[3,256,384]{2,1,0:T(8,128)(2,1)S(1)} %collective-permute-done.1.refs_2_, bf16[3,256,384]{2,1,0:T(8,128)(2,1)S(1)} %collective-permute-done.2.refs_3_), custom_call_target="tpu_custom_call" | custom-call | tf_op jit(solution)/shard_map/third_parts/pallas_call | solution.py:234
  175.3 6.5 %collective-permute-done.5.left_ref = bf16[3,256,384]{2,1,0:T(8,128)(2,1)S(1)} collective-permute-done((bf16[3,256,384]{2,1,0:T(8,128)(2,1)S(1)}, bf16[3,256,384]{2,1,0:T(8,128)(2,1)S(1)}, u32[]{:S(2)}, u32[]{:S(2)}) %collective-permute-start.5) | collective-permute-done | bytes 589856 | tf_op jit(solution)/shard_map/ppermute | solution.py:244
  181.8 1.2 collective-permute-done.6.right_ref
  183.0 1.3 finish.1
  184.3 1.1 all-to-all-done.1
  185.4 0.0 copy-done.1
  185.4 0.0 copy-done.2
  185.4 0.0 copy-done.3
  185.4 1.3 combine.1
Async XLA Ops:
  4.6 106.0 %all-to-all-start = ((bf16[32,32,2048]{2,1,0:T(8,128)(2,1)}), bf16[32,32,2048]{2,1,0:T(8,128)(2,1)}, u32[]{:S(2)}, u32[]{:S(2)}) async-start(bf16[32,32,2048]{2,1,0:T(8,128)(2,1)} %get-tuple-element.26), calls=%async_computation | async-start | bytes 8388608 | tf_op jit(solution)/shard_map/all_to_all | solution.py:335
  125.0 8.3 %collective-permute-start = (bf16[6,32,16,768]{3,2,1,0:T(8,128)(2,1)}, bf16[6,32,16,768]{3,2,1,0:T(8,128)(2,1)}, u32[]{:S(2)}, u32[]{:S(2)}) collective-permute-start(bf16[6,32,16,768]{3,2,1,0:T(8,128)(2,1)} %get-tuple-element.28), channel_id=1, source_target_pairs={{0,32},{32,0},{64,96},{96,64},{128,160},{160,128},{192,224},{224,1... | collective-permute-start | bytes 14155784 | tf_op jit(solution)/shard_map/ppermute | solution.py:243
  125.1 60.2 %all-to-all-start.1 = ((bf16[32,16,2176]{2,1,0:T(8,128)(2,1)}), bf16[32,16,2176]{2,1,0:T(8,128)(2,1)S(1)}, u32[]{:S(2)}, u32[]{:S(2)}) async-start(bf16[32,16,2176]{2,1,0:T(8,128)(2,1)} %bitcast.19), calls=%async_computation.1 | async-start | bytes 4456448 | tf_op jit(solution)/shard_map/all_to_all | solution.py:335
  133.3 2.3 %copy-start = (bf16[6,32,16,768]{3,2,1,0:T(8,128)(2,1)S(1)}, bf16[6,32,16,768]{3,2,1,0:T(8,128)(2,1)}, u32[]{:S(2)}) copy-start(bf16[6,32,16,768]{3,2,1,0:T(8,128)(2,1)} %get-tuple-element.27.refs_0_) | copy-start | bytes 14155780
  141.1 16.3 %collective-permute-start.3 = (bf16[3,256,384]{2,1,0:T(8,128)(2,1)S(1)}, bf16[3,256,384]{2,1,0:T(8,128)(2,1)S(1)}, u32[]{:S(2)}, u32[]{:S(2)}) collective-permute-start(bf16[3,256,384]{2,1,0:T(8,128)(2,1)S(1)} %get-tuple-element.31), channel_id=1, source_target_pairs={{0,64},{32,96},{64,128},{96,160},{128,192},{160,224},{192,0},{224,... | collective-permute-start | bytes 1769480 | tf_op jit(solution)/shard_map/ppermute | solution.py:244
  142.6 16.2 %collective-permute-start.4 = (bf16[3,256,384]{2,1,0:T(8,128)(2,1)S(1)}, bf16[3,256,384]{2,1,0:T(8,128)(2,1)S(1)}, u32[]{:S(2)}, u32[]{:S(2)}) collective-permute-start(bf16[3,256,384]{2,1,0:T(8,128)(2,1)S(1)} %get-tuple-element.32), channel_id=1, source_target_pairs={{0,192},{32,224},{64,0},{96,32},{128,64},{160,96},{192,128},{224,1... | collective-permute-start | bytes 1769480 | tf_op jit(solution)/shard_map/ppermute | solution.py:244
  143.2 26.8 %collective-permute-start.1 = (bf16[3,256,384]{2,1,0:T(8,128)(2,1)S(1)}, bf16[3,256,384]{2,1,0:T(8,128)(2,1)S(1)}, u32[]{:S(2)}, u32[]{:S(2)}) collective-permute-start(bf16[3,256,384]{2,1,0:T(8,128)(2,1)S(1)} %get-tuple-element.29), channel_id=1, source_target_pairs={{0,64},{32,96},{64,128},{96,160},{128,192},{160,224},{192,0},{224,... | collective-permute-start | bytes 1769480 | tf_op jit(solution)/shard_map/ppermute | solution.py:244
  144.7 26.8 %collective-permute-start.2 = (bf16[3,256,384]{2,1,0:T(8,128)(2,1)S(1)}, bf16[3,256,384]{2,1,0:T(8,128)(2,1)S(1)}, u32[]{:S(2)}, u32[]{:S(2)}) collective-permute-start(bf16[3,256,384]{2,1,0:T(8,128)(2,1)S(1)} %get-tuple-element.30), channel_id=1, source_target_pairs={{0,192},{32,224},{64,0},{96,32},{128,64},{160,96},{192,128},{224,1... | collective-permute-start | bytes 1769480 | tf_op jit(solution)/shard_map/ppermute | solution.py:244
  163.0 18.8 %collective-permute-start.5 = (bf16[3,256,384]{2,1,0:T(8,128)(2,1)S(1)}, bf16[3,256,384]{2,1,0:T(8,128)(2,1)S(1)}, u32[]{:S(2)}, u32[]{:S(2)}) collective-permute-start(bf16[3,256,384]{2,1,0:T(8,128)(2,1)S(1)} %get-tuple-element.33), channel_id=1, source_target_pairs={{0,64},{32,96},{64,128},{96,160},{128,192},{160,224},{192,0},{224,... | collective-permute-start | bytes 1769480 | tf_op jit(solution)/shard_map/ppermute | solution.py:244
  164.3 21.0 %copy-start.1 = (bf16[512,128]{1,0:T(8,128)(2,1)S(1)}, bf16[512,128]{1,0:T(8,128)(2,1)}, u32[]{:S(2)}) copy-start(bf16[512,128]{1,0:T(8,128)(2,1)} %get-tuple-element.38.s_ref) | copy-start | bytes 393220
  164.3 21.0 %copy-start.2 = (s32[128,8]{0,1:T(8,128)S(1)}, s32[128,8]{0,1:T(8,128)}, u32[]{:S(2)}) copy-start(s32[128,8]{0,1:T(8,128)} %param.9) | copy-start | bytes 12292
  164.3 21.0 %copy-start.3 = (bf16[128,8]{0,1:T(8,128)(2,1)S(1)}, bf16[128,8]{0,1:T(8,128)(2,1)}, u32[]{:S(2)}) copy-start(bf16[128,8]{0,1:T(8,128)(2,1)} %param.10) | copy-start | bytes 6148
  164.3 18.7 %collective-permute-start.6 = (bf16[3,256,384]{2,1,0:T(8,128)(2,1)S(1)}, bf16[3,256,384]{2,1,0:T(8,128)(2,1)S(1)}, u32[]{:S(2)}, u32[]{:S(2)}) collective-permute-start(bf16[3,256,384]{2,1,0:T(8,128)(2,1)S(1)} %get-tuple-element.34), channel_id=1, source_target_pairs={{0,192},{32,224},{64,0},{96,32},{128,64},{160,96},{192,128},{224,1... | collective-permute-start | bytes 1769480 | tf_op jit(solution)/shard_map/ppermute | solution.py:244

commit v5 on v4

--- a/solution.py
+++ b/solution.py
@@ -182,7 +182,7 @@
             pltpu.SemaphoreType.DMA((4,)),
             pltpu.SemaphoreType.DMA((18,)),
         ],
-        compiler_params=params(),
+        compiler_params=params(50 * 1024 * 1024),
         cost_estimate=cost(10 * rows * width * hid, 2 * (3 * rows * width + 3 * width * hid)),
         name="rows_pass",
     )(place, recv, wg, wu, wd)

time: 187 us -> 189 us (1.011)
  no operation moved by 1% of the time
where the time goes in v5:
time: 189 us; the launch traced here: 188 us
  waiting for transfers between devices  124 us (66%)
  Pallas kernels  34.8 us (18%)
  starting transfers between devices  24.8 us (13%)
  local copies, waits for them, and re-layouts  3.81 us (2%)
    all_to_all x2, waiting for transfers between devices, exchange(): lax.all_to_all(rows, 'expert', split_axis=0, concat_axis=0, tiled=True)  95.3 us
    ppermute x6, waiting for transfers between devices, reduce_parts(): lax.ppermute(t, 'dp', [(i, (i + 2 * d) % 8) for i in range(8)])  27.7 us
    all_to_all x2, starting transfers between devices, exchange(): lax.all_to_all(rows, 'expert', split_axis=0, concat_axis=0, tiled=True)  18.6 us
    pallas_call x1, Pallas kernels, rows_pass(): pl.pallas_call(rows_kernel, in_specs=[pl.BlockSpec(memory_space=pltpu.SME...  14.9 us
    pallas_call x3, Pallas kernels, part_call(): pl.pallas_call(kernel, out_shape=outs, compiler_params=params(20 * 1024 *...  13.3 us
    ppermute x6, starting transfers between devices, reduce_parts(): lax.ppermute(t, 'dp', [(i, (i + 2 * d) % 8) for i in range(8)])  6.23 us
    pallas_call x1, Pallas kernels, route(): pl.pallas_call(functools.partial(route_kernel, groups), grid=(steps,), in...  4.04 us
  transfers between devices with their start and end apart: 9, of which 9 were waited for; matrix products, arithmetic and copies ran while one was open for 0% of the time, Pallas kernels for 8%

profile of v5, /device:TPU:2, one launch (start us, length us, event | category | flops | bytes accessed | tf_op | source)
XLA Modules:
  0.0 188.5 jit_solution(4699841165767204576)
XLA Ops:
  0.6 4.0 %route.1 = (bf16[32,32,2048]{2,1,0:T(8,128)(2,1)}, bf16[512,128]{1,0:T(8,128)(2,1)}) custom-call(s32[8,128]{1,0:T(8,128)} %bitcast.16, bf16[8,128]{1,0:T(8,128)(2,1)} %bitcast.18, bf16[128,2048]{1,0:T(8,128)(2,1)} %tok_ref.1, bf16[128,2048]{1,0:T(8,128)(2,1)} %dy_ref.1), custom_call_target="tpu_custom_call" | custom-call | flops 536870912 | bytes 5242880 | tf_op jit(solution)/shard_map/route/pallas_call | solution.py:75
  4.7 11.6 %all-to-all-start = ((bf16[32,32,2048]{2,1,0:T(8,128)(2,1)}), bf16[32,32,2048]{2,1,0:T(8,128)(2,1)}, u32[]{:S(2)}, u32[]{:S(2)}) async-start(bf16[32,32,2048]{2,1,0:T(8,128)(2,1)} %get-tuple-element.26), calls=%async_computation | async-start | bytes 8388608 | tf_op jit(solution)/shard_map/all_to_all | solution.py:335
  16.4 0.1 stack.23.place_ref
  16.5 94.2 %all-to-all-done.recv_hbm = bf16[32,32,2048]{2,1,0:T(8,128)(2,1)} async-done(((bf16[32,32,2048]{2,1,0:T(8,128)(2,1)}), bf16[32,32,2048]{2,1,0:T(8,128)(2,1)}, u32[]{:S(2)}, u32[]{:S(2)}) %all-to-all-start) | async-done | bytes 4194336 | tf_op jit(solution)/shard_map/all_to_all | solution.py:335
  110.6 14.9 %rows_pass.1 = (bf16[512,2176]{1,0:T(8,128)(2,1)S(1)}, bf16[6,32,16,768]{3,2,1,0:T(8,128)(2,1)}, bf16[6,32,16,768]{3,2,1,0:T(8,128)(2,1)}) custom-call(s32[5]{0:T(128)S(1)} %stack.23.place_ref, bf16[32,32,2048]{2,1,0:T(8,128)(2,1)} %all-to-all-done.recv_hbm, bf16[2048,768]{1,0:T(8,128)(2,1)} %bitcast.20, bf16[2048,768]{1,0:T(8,128)(2,1)} %bitcast.21, ...), custom_call_target="tpu_custom_call" | custom-call | flops 8053063680 | bytes 15728640 | tf_op jit(solution)/shard_map/rows_pass/pallas_call | solution.py:168
  125.6 0.0 copy-start.1
  125.6 1.4 copy-done.1
  127.0 0.0 collective-permute-start
  127.0 7.0 %all-to-all-start.1 = ((bf16[32,16,2176]{2,1,0:T(8,128)(2,1)}), bf16[32,16,2176]{2,1,0:T(8,128)(2,1)S(1)}, u32[]{:S(2)}, u32[]{:S(2)}) async-start(bf16[32,16,2176]{2,1,0:T(8,128)(2,1)} %bitcast.15), calls=%async_computation.1 | async-start | bytes 4456448 | tf_op jit(solution)/shard_map/all_to_all | solution.py:335
  133.9 1.3 collective-permute-done.refs_1_
  135.2 0.0 copy-start
  135.2 2.3 %copy-done = bf16[6,32,16,768]{3,2,1,0:T(8,128)(2,1)S(1)} copy-done((bf16[6,32,16,768]{3,2,1,0:T(8,128)(2,1)S(1)}, bf16[6,32,16,768]{3,2,1,0:T(8,128)(2,1)}, u32[]{:S(2)}) %copy-start) | copy-done | bytes 4718616
  137.5 5.4 %first_parts.1 = (bf16[3,256,384]{2,1,0:T(8,128)(2,1)S(1)}, bf16[3,256,384]{2,1,0:T(8,128)(2,1)S(1)}, bf16[3,256,384]{2,1,0:T(8,128)(2,1)S(1)}, bf16[3,256,384]{2,1,0:T(8,128)(2,1)S(1)}) custom-call(bf16[6,32,16,768]{3,2,1,0:T(8,128)(2,1)S(1)} %copy-done, bf16[6,32,16,768]{3,2,1,0:T(8,128)(2,1)} %collective-permute-done.refs_1_), custom_call_target="tpu_custom_call" | custom-call | tf_op jit(solution)/shard_map/first_parts/pallas_call | solution.py:234
  142.9 1.6 collective-permute-start.3
  144.5 0.5 collective-permute-start.4
  145.0 1.5 collective-permute-start.1
  146.5 0.5 collective-permute-start.2
  147.1 12.1 %collective-permute-done.3.refs_2_ = bf16[3,256,384]{2,1,0:T(8,128)(2,1)S(1)} collective-permute-done((bf16[3,256,384]{2,1,0:T(8,128)(2,1)S(1)}, bf16[3,256,384]{2,1,0:T(8,128)(2,1)S(1)}, u32[]{:S(2)}, u32[]{:S(2)}) %collective-permute-start.3) | collective-permute-done | bytes 589856 | tf_op jit(solution)/shard_map/ppermute | solution.py:244
  159.2 1.5 collective-permute-done.4.refs_3_
  160.7 4.2 %second_parts.1 = (bf16[3,256,384]{2,1,0:T(8,128)(2,1)S(1)}, bf16[3,256,384]{2,1,0:T(8,128)(2,1)S(1)}) custom-call(bf16[6,32,16,768]{3,2,1,0:T(8,128)(2,1)S(1)} %copy-done, bf16[6,32,16,768]{3,2,1,0:T(8,128)(2,1)} %collective-permute-done.refs_1_, bf16[3,256,384]{2,1,0:T(8,128)(2,1)S(1)} %collective-permute-done.3.refs_2_, ...), custom_call_target="tpu_custom_call" | custom-call | tf_op jit(solution)/shard_map/second_parts/pallas_call | solution.py:234
  164.9 1.3 collective-permute-start.5
  166.2 0.0 copy-start.2
  166.2 0.0 copy-start.3
  166.2 0.0 copy-start.4
  166.2 0.8 collective-permute-start.6
  167.0 4.8 %collective-permute-done.1.refs_2_ = bf16[3,256,384]{2,1,0:T(8,128)(2,1)S(1)} collective-permute-done((bf16[3,256,384]{2,1,0:T(8,128)(2,1)S(1)}, bf16[3,256,384]{2,1,0:T(8,128)(2,1)S(1)}, u32[]{:S(2)}, u32[]{:S(2)}) %collective-permute-start.1) | collective-permute-done | bytes 589856 | tf_op jit(solution)/shard_map/ppermute | solution.py:244
  171.8 1.5 collective-permute-done.2.refs_3_
  173.4 3.8 %third_parts.1.sum_ref = bf16[2,3,256,384]{3,2,1,0:T(8,128)(2,1)S(1)} custom-call(bf16[6,32,16,768]{3,2,1,0:T(8,128)(2,1)S(1)} %copy-done, bf16[6,32,16,768]{3,2,1,0:T(8,128)(2,1)} %collective-permute-done.refs_1_, bf16[3,256,384]{2,1,0:T(8,128)(2,1)S(1)} %collective-permute-done.1.refs_2_, bf16[3,256,384]{2,1,0:T(8,128)(2,1)S(1)} %collective-permute-done.2.refs_3_), custom_call_target="tpu_custom_call" | custom-call | tf_op jit(solution)/shard_map/third_parts/pallas_call | solution.py:234
  177.1 6.6 %collective-permute-done.5.left_ref = bf16[3,256,384]{2,1,0:T(8,128)(2,1)S(1)} collective-permute-done((bf16[3,256,384]{2,1,0:T(8,128)(2,1)S(1)}, bf16[3,256,384]{2,1,0:T(8,128)(2,1)S(1)}, u32[]{:S(2)}, u32[]{:S(2)}) %collective-permute-start.5) | collective-permute-done | bytes 589856 | tf_op jit(solution)/shard_map/ppermute | solution.py:244
  183.7 1.2 collective-permute-done.6.right_ref
  184.9 1.3 finish.1
  186.1 1.1 all-to-all-done.1
  187.2 0.0 copy-done.2
  187.2 0.0 copy-done.3
  187.2 0.0 copy-done.4
  187.2 1.3 combine.1
Async XLA Ops:
  4.7 106.0 %all-to-all-start = ((bf16[32,32,2048]{2,1,0:T(8,128)(2,1)}), bf16[32,32,2048]{2,1,0:T(8,128)(2,1)}, u32[]{:S(2)}, u32[]{:S(2)}) async-start(bf16[32,32,2048]{2,1,0:T(8,128)(2,1)} %get-tuple-element.26), calls=%async_computation | async-start | bytes 8388608 | tf_op jit(solution)/shard_map/all_to_all | solution.py:335
  125.6 1.4 copy-start.1
  127.0 8.3 %collective-permute-start = (bf16[6,32,16,768]{3,2,1,0:T(8,128)(2,1)}, bf16[6,32,16,768]{3,2,1,0:T(8,128)(2,1)}, u32[]{:S(2)}, u32[]{:S(2)}) collective-permute-start(bf16[6,32,16,768]{3,2,1,0:T(8,128)(2,1)} %get-tuple-element.28), channel_id=1, source_target_pairs={{0,32},{32,0},{64,96},{96,64},{128,160},{160,128},{192,224},{224,1... | collective-permute-start | bytes 14155784 | tf_op jit(solution)/shard_map/ppermute | solution.py:243
  127.0 60.2 %all-to-all-start.1 = ((bf16[32,16,2176]{2,1,0:T(8,128)(2,1)}), bf16[32,16,2176]{2,1,0:T(8,128)(2,1)S(1)}, u32[]{:S(2)}, u32[]{:S(2)}) async-start(bf16[32,16,2176]{2,1,0:T(8,128)(2,1)} %bitcast.15), calls=%async_computation.1 | async-start | bytes 4456448 | tf_op jit(solution)/shard_map/all_to_all | solution.py:335
  135.2 2.3 %copy-start = (bf16[6,32,16,768]{3,2,1,0:T(8,128)(2,1)S(1)}, bf16[6,32,16,768]{3,2,1,0:T(8,128)(2,1)}, u32[]{:S(2)}) copy-start(bf16[6,32,16,768]{3,2,1,0:T(8,128)(2,1)} %get-tuple-element.27.refs_0_) | copy-start | bytes 14155780
  142.9 16.3 %collective-permute-start.3 = (bf16[3,256,384]{2,1,0:T(8,128)(2,1)S(1)}, bf16[3,256,384]{2,1,0:T(8,128)(2,1)S(1)}, u32[]{:S(2)}, u32[]{:S(2)}) collective-permute-start(bf16[3,256,384]{2,1,0:T(8,128)(2,1)S(1)} %get-tuple-element.31), channel_id=1, source_target_pairs={{0,64},{32,96},{64,128},{96,160},{128,192},{160,224},{192,0},{224,... | collective-permute-start | bytes 1769480 | tf_op jit(solution)/shard_map/ppermute | solution.py:244
  144.5 16.2 %collective-permute-start.4 = (bf16[3,256,384]{2,1,0:T(8,128)(2,1)S(1)}, bf16[3,256,384]{2,1,0:T(8,128)(2,1)S(1)}, u32[]{:S(2)}, u32[]{:S(2)}) collective-permute-start(bf16[3,256,384]{2,1,0:T(8,128)(2,1)S(1)} %get-tuple-element.32), channel_id=1, source_target_pairs={{0,192},{32,224},{64,0},{96,32},{128,64},{160,96},{192,128},{224,1... | collective-permute-start | bytes 1769480 | tf_op jit(solution)/shard_map/ppermute | solution.py:244
  145.0 26.8 %collective-permute-start.1 = (bf16[3,256,384]{2,1,0:T(8,128)(2,1)S(1)}, bf16[3,256,384]{2,1,0:T(8,128)(2,1)S(1)}, u32[]{:S(2)}, u32[]{:S(2)}) collective-permute-start(bf16[3,256,384]{2,1,0:T(8,128)(2,1)S(1)} %get-tuple-element.29), channel_id=1, source_target_pairs={{0,64},{32,96},{64,128},{96,160},{128,192},{160,224},{192,0},{224,... | collective-permute-start | bytes 1769480 | tf_op jit(solution)/shard_map/ppermute | solution.py:244
  146.5 26.8 %collective-permute-start.2 = (bf16[3,256,384]{2,1,0:T(8,128)(2,1)S(1)}, bf16[3,256,384]{2,1,0:T(8,128)(2,1)S(1)}, u32[]{:S(2)}, u32[]{:S(2)}) collective-permute-start(bf16[3,256,384]{2,1,0:T(8,128)(2,1)S(1)} %get-tuple-element.30), channel_id=1, source_target_pairs={{0,192},{32,224},{64,0},{96,32},{128,64},{160,96},{192,128},{224,1... | collective-permute-start | bytes 1769480 | tf_op jit(solution)/shard_map/ppermute | solution.py:244
  164.9 18.8 %collective-permute-start.5 = (bf16[3,256,384]{2,1,0:T(8,128)(2,1)S(1)}, bf16[3,256,384]{2,1,0:T(8,128)(2,1)S(1)}, u32[]{:S(2)}, u32[]{:S(2)}) collective-permute-start(bf16[3,256,384]{2,1,0:T(8,128)(2,1)S(1)} %get-tuple-element.33), channel_id=1, source_target_pairs={{0,64},{32,96},{64,128},{96,160},{128,192},{160,224},{192,0},{224,... | collective-permute-start | bytes 1769480 | tf_op jit(solution)/shard_map/ppermute | solution.py:244
  166.2 21.0 %copy-start.2 = (bf16[512,128]{1,0:T(8,128)(2,1)S(1)}, bf16[512,128]{1,0:T(8,128)(2,1)}, u32[]{:S(2)}) copy-start(bf16[512,128]{1,0:T(8,128)(2,1)} %get-tuple-element.38.s_ref) | copy-start | bytes 393220
  166.2 21.0 %copy-start.3 = (s32[128,8]{0,1:T(8,128)S(1)}, s32[128,8]{0,1:T(8,128)}, u32[]{:S(2)}) copy-start(s32[128,8]{0,1:T(8,128)} %param.9) | copy-start | bytes 12292
  166.2 21.0 %copy-start.4 = (bf16[128,8]{0,1:T(8,128)(2,1)S(1)}, bf16[128,8]{0,1:T(8,128)(2,1)}, u32[]{:S(2)}) copy-start(bf16[128,8]{0,1:T(8,128)(2,1)} %param.10) | copy-start | bytes 6148
  166.2 18.7 %collective-permute-start.6 = (bf16[3,256,384]{2,1,0:T(8,128)(2,1)S(1)}, bf16[3,256,384]{2,1,0:T(8,128)(2,1)S(1)}, u32[]{:S(2)}, u32[]{:S(2)}) collective-permute-start(bf16[3,256,384]{2,1,0:T(8,128)(2,1)S(1)} %get-tuple-element.34), channel_id=1, source_target_pairs={{0,192},{32,224},{64,0},{96,32},{128,64},{160,96},{192,128},{224,1... | collective-permute-start | bytes 1769480 | tf_op jit(solution)/shard_map/ppermute | solution.py:244
